TPU v7x, 256 devices: a whole 4x4x8 slice. The times are simulated.
256 devices in a mesh: ctx: 32 (over z_hi, x, core), head: 8 (over z_lo, y).
Axes of the slice: x: 4, y: 4, z: 8 (z_hi: 4, z_lo: 2; z = z_hi * 2 + z_lo), core: 2. Of those that a mesh axis runs over, the one named last changes fastest.
Arguments:
- block_order: int32 [32], replicated, may hold values from 0 to 31, each once
- queries: bfloat16 [4096, 4096], P('ctx', 'head'), may hold values from -36 to 36
- latent: bfloat16 [4096, 512], P('ctx'), may hold values from -6 to 6
- rope_keys: bfloat16 [4096, 128], P('ctx'), may hold values from -12 to 12
- w_uk: bfloat16 [512, 3584], P(None, 'head'), may hold values from -0.25 to 0.25
- w_uv: bfloat16 [512, 4096], P(None, 'head'), may hold values from -0.25 to 0.25
- cotangent: bfloat16 [4096, 4096], P('ctx', 'head'), may hold values from -6 to 6
- attn_out: bfloat16 [4096, 4096], P('ctx', 'head'), may hold values from -6 to 6
Outputs:
- d_queries: bfloat16 [4096, 4096], P('ctx', 'head')
- d_latent: float32 [4096, 512], P('ctx')
- d_rope_keys: float32 [4096, 128], P('ctx')
- d_w_uk: float32 [512, 3584], P('ctx', 'head')
Inputs may be any that keep to these rules, and one draw needn't show every extreme that they name: A permutation of the blocks; index i of ctx holds the positions block_order[i] * 128 to block_order[i] * 128 + 127 of the window.
All inputs are finite; a program needn't handle non-finite values.
Results may differ from a plain program's by a relative error of at most 0.0075.
Values may be sent and summed in bfloat16 or wider, within the bound.
A program may use at most 128 MiB of HBM per device.

v0:
```python
import math

import jax
import jax.numpy as jnp
from jax import lax
from jax.sharding import PartitionSpec as P

H = 32
KVG = 8
NOPE = 112
ROPE = 16
VD = 128


negative_fill = -1e30


def lookup_order(block_order, block_ids):
    listed = jnp.arange(block_order.shape[0], dtype=jnp.int32)
    hits = block_ids[:, None] == listed[None, :]
    return jnp.sum(jnp.where(hits, block_order[None, :], 0), axis=1)


def key_positions(block_order, begin_row, row_count, tok_rows):
    row_ids = begin_row + jnp.arange(row_count, dtype=jnp.int32)
    return lookup_order(block_order, row_ids // tok_rows) * tok_rows + row_ids % tok_rows


def on_device(block_order, queries, latent, rope_keys, w_uk, w_uv, cotangent, attn_out):
    tok_rows = queries.shape[0]
    head_width = NOPE + ROPE
    local_heads = queries.shape[1] // head_width
    rank_width = latent.shape[1]
    rope_cols = rope_keys.shape[1]
    scale_factor = 1.0 / math.sqrt(head_width)
    my_block = lookup_order(block_order, jnp.reshape(lax.axis_index("ctx"), (1,)))[0]
    query_pos = my_block * tok_rows + jnp.arange(tok_rows, dtype=jnp.int32)
    head_ids = lax.axis_index("head") * local_heads + jnp.arange(local_heads, dtype=jnp.int32)
    group_ids = jnp.arange(KVG, dtype=jnp.int32)
    selector = (head_ids[:, None] // (H // KVG) == group_ids[None, :]).astype(jnp.bfloat16)
    selector_wide = selector.astype(jnp.float32)
    query_three = queries.reshape(tok_rows, local_heads, head_width)
    query_nope = query_three[:, :, :NOPE]
    query_rope = jnp.transpose(query_three[:, :, NOPE:], (1, 0, 2))
    uk_three = w_uk.reshape(rank_width, local_heads, NOPE)
    uv_three = w_uv.reshape(rank_width, local_heads, VD)
    cot_three = cotangent.reshape(tok_rows, local_heads, VD)
    saved_three = attn_out.reshape(tok_rows, local_heads, VD)
    query_lat = jnp.einsum(
        "thd,rhd->htr", query_nope, uk_three, preferred_element_type=jnp.float32
    ).astype(jnp.bfloat16)
    out_lat = jnp.einsum(
        "the,rhe->htr", cot_three, uv_three, preferred_element_type=jnp.float32
    ).astype(jnp.bfloat16)
    delta = jnp.transpose(
        jnp.sum(cot_three.astype(jnp.float32) * saved_three.astype(jnp.float32), axis=2)
    )

    def head_rope(rope_piece):
        grouped = rope_piece.reshape(rope_piece.shape[0], KVG, ROPE)
        return jnp.einsum(
            "kgd,hg->khd", grouped, selector, preferred_element_type=jnp.float32
        ).astype(jnp.bfloat16)

    def block_scores(lat_piece, rope_heads, begin_row):
        key_pos = key_positions(block_order, begin_row, lat_piece.shape[0], tok_rows)
        allowed = key_pos[None, :] <= query_pos[:, None]
        nope_part = jnp.einsum(
            "htr,kr->htk", query_lat, lat_piece, preferred_element_type=jnp.float32
        )
        rope_part = jnp.einsum(
            "htd,khd->htk", query_rope, rope_heads, preferred_element_type=jnp.float32
        )
        scores = (nope_part + rope_part) * scale_factor
        return jnp.where(allowed[None], scores, negative_fill)

    def stats_step(carry, lat_piece, rope_piece, begin_row):
        running_max, running_sum = carry
        scores = block_scores(lat_piece, head_rope(rope_piece), begin_row)
        new_max = jnp.maximum(running_max, jnp.max(scores, axis=2))
        running_sum = running_sum * jnp.exp(running_max - new_max) + jnp.sum(
            jnp.exp(scores - new_max[:, :, None]), axis=2
        )
        return (new_max, running_sum)

    stats_init = (
        jnp.full((local_heads, tok_rows), negative_fill, jnp.float32),
        jnp.zeros((local_heads, tok_rows), jnp.float32),
    )
    total_rows = tok_rows * lax.axis_size("ctx")
    whole_lat, whole_rope = (
        lax.all_gather(latent, "ctx", axis=0, tiled=True),
        lax.all_gather(rope_keys, "ctx", axis=0, tiled=True),
    )
    span = math.gcd(total_rows, 512)
    block_total = total_rows // span

    def stats_loop(block_index, carry):
        begin_row = block_index * span
        return stats_step(
            carry,
            lax.dynamic_slice_in_dim(whole_lat, begin_row, span, 0),
            lax.dynamic_slice_in_dim(whole_rope, begin_row, span, 0),
            begin_row,
        )

    running_max, running_sum = lax.fori_loop(0, block_total, stats_loop, stats_init)
    log_total = running_max + jnp.log(running_sum)

    def grad_step(carry, lat_piece, rope_piece, begin_row):
        lat_sum, rope_sum, lat_grad, rope_grad = carry
        row_count = lat_piece.shape[0]
        rope_heads = head_rope(rope_piece)
        scores = block_scores(lat_piece, rope_heads, begin_row)
        weights = jnp.exp(scores - log_total[:, :, None])
        dots = jnp.einsum("htr,kr->htk", out_lat, lat_piece, preferred_element_type=jnp.float32)
        grad_scores = (weights * (dots - delta[:, :, None]) * scale_factor).astype(jnp.bfloat16)
        probs = weights.astype(jnp.bfloat16)
        lat_sum = lat_sum + jnp.einsum(
            "htk,kr->htr", grad_scores, lat_piece, preferred_element_type=jnp.float32
        )
        rope_sum = rope_sum + jnp.einsum(
            "htk,khd->htd", grad_scores, rope_heads, preferred_element_type=jnp.float32
        )
        lat_block = jnp.einsum(
            "htk,htr->kr", grad_scores, query_lat, preferred_element_type=jnp.float32
        ) + jnp.einsum("htk,htr->kr", probs, out_lat, preferred_element_type=jnp.float32)
        rope_block = jnp.einsum(
            "htk,htd->khd", grad_scores, query_rope, preferred_element_type=jnp.float32
        )
        rope_block = jnp.einsum(
            "khd,hg->kgd", rope_block, selector_wide, precision=lax.Precision.HIGHEST
        ).reshape(row_count, rope_cols)
        lat_grad = lax.dynamic_update_slice_in_dim(lat_grad, lat_block, begin_row, 0)
        rope_grad = lax.dynamic_update_slice_in_dim(rope_grad, rope_block, begin_row, 0)
        return (lat_sum, rope_sum, lat_grad, rope_grad)

    grad_init = (
        jnp.zeros((local_heads, tok_rows, rank_width), jnp.float32),
        jnp.zeros((local_heads, tok_rows, ROPE), jnp.float32),
        jnp.zeros((total_rows, rank_width), jnp.float32),
        jnp.zeros((total_rows, rope_cols), jnp.float32),
    )

    def grad_loop(block_index, carry):
        begin_row = block_index * span
        return grad_step(
            carry,
            lax.dynamic_slice_in_dim(whole_lat, begin_row, span, 0),
            lax.dynamic_slice_in_dim(whole_rope, begin_row, span, 0),
            begin_row,
        )

    lat_sum, rope_sum, lat_grad, rope_grad = lax.fori_loop(0, block_total, grad_loop, grad_init)
    dq_lat = lat_sum.astype(jnp.bfloat16)
    dq_nope = jnp.einsum("htr,rhd->thd", dq_lat, uk_three, preferred_element_type=jnp.float32)
    dq_rope = jnp.transpose(rope_sum, (1, 0, 2))
    d_queries = jnp.concatenate([dq_nope, dq_rope], axis=2).astype(jnp.bfloat16)
    d_queries = d_queries.reshape(tok_rows, local_heads * head_width)
    weight_part = jnp.einsum(
        "htr,thd->rhd", dq_lat, query_nope, preferred_element_type=jnp.float32
    ).reshape(rank_width, local_heads * NOPE)
    lat_mine, rope_mine, weight_grad = (
        lax.psum_scatter(lat_grad, "ctx", scatter_dimension=0, tiled=True),
        lax.psum_scatter(rope_grad, "ctx", scatter_dimension=0, tiled=True),
        lax.psum_scatter(weight_part, "ctx", scatter_dimension=0, tiled=True),
    )
    d_latent, d_rope = lax.psum((lat_mine, rope_mine), "head")
    return (d_queries, d_latent, d_rope, weight_grad)


def solution(mesh):
    return jax.shard_map(
        on_device,
        mesh=mesh,
        in_specs=(
            P(),
            P("ctx", "head"),
            P("ctx", None),
            P("ctx", None),
            P(None, "head"),
            P(None, "head"),
            P("ctx", "head"),
            P("ctx", "head"),
        ),
        out_specs=(P("ctx", "head"), P("ctx", None), P("ctx", None), P("ctx", "head")),
        check_vma=False,
    )
```

profile of v0, /device:TPU:32, one launch (start us, length us, event | category | flops | bytes accessed | tf_op | source)
XLA Modules:
  0.0 663.4 jit_solution(14749283632022487272)
XLA Ops:
  7.2 1.5 copy.63
  17.4 47.0 %all-gather.5.cloned.1.call-done = bf16[4096,128]{0,1:T(8,128)(2,1)} async-done(((bf16[128,128]{0,1:T(8,128)(2,1)}), bf16[4096,128]{0,1:T(8,128)(2,1)}) %all-gather.5.cloned.1.call-update) | async-done | bytes 1048592 | tf_op jit(solution)/shard_map/all_gather | solution.py:93
  64.4 60.3 %all-gather.3.cloned.1.call-done = bf16[4096,512]{1,0:T(8,128)(2,1)} async-done(((bf16[128,512]{1,0:T(8,128)(2,1)}), bf16[4096,512]{1,0:T(8,128)(2,1)}) %all-gather.3.cloned.1.call-update) | async-done | bytes 4194320 | tf_op jit(solution)/shard_map/all_gather | solution.py:92
  124.7 33.9 %while.42 = (s32[]{:T(128)}, f32[4,128]{1,0:T(4,128)S(1)}, f32[4,128]{1,0:T(4,128)S(1)}, s32[32]{0:T(128)}, bf16[4096,512]{1,0:T(8,128)(2,1)}, /*index=5*/bf16[4...) while((s32[]{:T(128)}, f32[4,128]{1,0:T(4,128)S(1)}, ...), condition=%wide.region_5.6_spmd.clone, body=%wide.region_1.0_spmd.clone.sunk | while | flops 279086272 | bytes 5954922 | solution.py:107
  126.8 1.5 convolution_bitcast_fusion.13
  131.0 1.5 convolution_bitcast_fusion.13
  135.3 1.5 convolution_bitcast_fusion.13
  139.5 1.5 convolution_bitcast_fusion.13
  143.8 1.5 convolution_bitcast_fusion.13
  148.0 1.5 convolution_bitcast_fusion.13
  152.2 1.5 convolution_bitcast_fusion.13
  156.5 1.5 convolution_bitcast_fusion.13
  158.6 1.5 broadcast_in_dim.192.clone
  160.1 4.3 broadcast_in_dim.191
  164.4 105.9 %while.43 = (s32[]{:T(128)}, f32[4,128,512]{2,1,0:T(8,128)}, f32[4,128,16]{1,2,0:T(8,128)S(1)}, f32[4096,512]{1,0:T(8,128)}, f32[4096,128]{1,0:T(8,128)}, /*inde...) while((s32[]{:T(128)}, f32[4,128,512]{2,1,0:T(8,128)}, ...), condition=%wide.region_9.10_spmd.clone.clone.clone, body=%wide.region_7.9_spmd.clone.clone.clone.sunk | while | flops 1374337920 | bytes 19711408 | solution.py:154
  165.8 1.5 convolution_bitcast_fusion.14
  167.8 1.5 fusion.159
  172.7 2.5 convolution_add_fusion.4
  178.8 1.5 convolution_bitcast_fusion.14
  180.8 1.5 fusion.159
  185.6 2.9 convolution_add_fusion.4
  189.2 1.5 fusion.160
  192.1 1.5 convolution_bitcast_fusion.14
  194.1 1.5 fusion.159
  198.9 2.9 convolution_add_fusion.4
  205.4 1.5 convolution_bitcast_fusion.14
  207.4 1.5 fusion.159
  212.2 2.9 convolution_add_fusion.4
  218.6 1.5 convolution_bitcast_fusion.14
  220.6 1.5 fusion.159
  225.5 2.9 convolution_add_fusion.4
  231.9 1.5 convolution_bitcast_fusion.14
  233.9 1.5 fusion.159
  238.7 2.9 convolution_add_fusion.4
  242.3 1.5 fusion.160
  245.2 1.5 convolution_bitcast_fusion.14
  247.2 1.5 fusion.159
  252.0 2.9 convolution_add_fusion.4
  255.6 1.4 fusion.160
  258.5 1.5 convolution_bitcast_fusion.14
  260.5 1.5 fusion.159
  265.3 2.9 convolution_add_fusion.4
  273.7 86.0 %reduce-scatter.6.cloned.1.call-done = f32[128,128]{1,0:T(8,128)} async-done(((f32[4096,128]{1,0:T(8,128)}), f32[128,128]{1,0:T(8,128)}) %reduce-scatter.6.cloned.1.call-update) | async-done | bytes 65552 | tf_op jit(solution)/shard_map/reduce_scatter | solution.py:165
  359.7 122.7 %reduce-scatter.4.cloned.1.call-done = f32[128,512]{1,0:T(8,128)} async-done(((f32[4096,512]{1,0:T(8,128)}), f32[128,512]{1,0:T(8,128)}) %reduce-scatter.4.cloned.1.call-update) | async-done | bytes 262160 | tf_op jit(solution)/shard_map/reduce_scatter | solution.py:164
  483.2 90.6 %reduce-scatter.8.cloned.1.call-done = f32[16,448]{1,0:T(8,128)} async-done(((f32[512,448]{1,0:T(8,128)}), f32[16,448]{1,0:T(8,128)}) %reduce-scatter.8.cloned.1.call-update) | async-done | bytes 28688 | tf_op jit(solution)/shard_map/reduce_scatter | solution.py:166
  573.8 79.6 %all-reduce.3.cloned.1.call-done = (f32[128,512]{1,0:T(8,128)}, f32[128,128]{1,0:T(8,128)}) async-done(((f32[128,512]{1,0:T(8,128)}, f32[128,128]{1,0:T(8,128)}), (f32[128,512]{1,0:T(8,128)}, f32[128,128]{1,0:T(8,128)})) %all-reduce.3.cloned.1.call-update) | async-done | bytes 327696 | tf_op jit(solution)/shard_map/psum | solution.py:168
  653.4 1.7 copy.144
  655.1 1.5 copy.145
  (266 shorter events, 87.5 us)
Async XLA Ops:
  7.2 9.0 %copy-start = (bf16[512,512]{1,0:T(8,128)(2,1)S(1)}, bf16[512,512]{1,0:T(8,128)(2,1)}, u32[]{:S(2)}) copy-start(bf16[512,512]{1,0:T(8,128)(2,1)} %param.17) | copy-start | bytes 1572868
  7.2 57.2 %all-gather.5.cloned.1.call-start = ((), (), s32[]{:S(2)}) async-start(), calls=%async_computation.4 | async-start | bytes 1081344 | tf_op jit(solution)/shard_map/all_gather | solution.py:93
  8.8 115.9 %all-gather.3.cloned.1.call-start = ((), (), s32[]{:S(2)}) async-start(), calls=%async_computation.3 | async-start | bytes 4325376 | tf_op jit(solution)/shard_map/all_gather | solution.py:92
  9.5 350.2 %reduce-scatter.6.cloned.1.call-start = ((), (), s32[]{:S(2)}) async-start(), calls=%async_computation.6 | async-start | bytes 2162688 | tf_op jit(solution)/shard_map/reduce_scatter | solution.py:165
  10.6 4.2 copy-start.3
  160.1 4.3 copy-start.5
  270.3 212.0 %reduce-scatter.4.cloned.1.call-start = ((), (), s32[]{:S(2)}) async-start(), calls=%async_computation.5 | async-start | bytes 8650752 | tf_op jit(solution)/shard_map/reduce_scatter | solution.py:164
  270.4 1.2 copy-start.1
  270.4 1.2 copy-start.4
  270.9 2.5 copy-start.2
  270.9 302.9 %reduce-scatter.8.cloned.1.call-start = ((), (), s32[]{:S(2)}) async-start(), calls=%async_computation.7 | async-start | bytes 1081344 | tf_op jit(solution)/shard_map/reduce_scatter | solution.py:166
  273.3 380.1 %all-reduce.3.cloned.1.call-start = ((), (), s32[]{:S(2)}) async-start(), calls=%async_computation.8 | async-start | bytes 655360 | tf_op jit(solution)/shard_map/psum | solution.py:168
Sparse Core Ops, SparseCore 0:
  11.1 53.2 all-gather.4
  66.9 57.7 all-gather.2
  270.5 89.1 reduce-scatter.5
  363.6 118.7 reduce-scatter.3
  487.0 86.7 reduce-scatter.7
  576.4 76.9 all-reduce.2
where the time goes:
time: 667 us; the launch traced here: 663 us
  waiting for transfers between devices  487 us (73%)
  matrix products  95 us (14%)
  local copies, waits for them, and re-layouts  52.3 us (8%)
  between operations  14.9 us (2%)
  other arithmetic  12.4 us (2%)
    reduce_scatter x1, waiting for transfers between devices, on_device(): lax.psum_scatter(lat_grad, 'ctx', scatter_dimension=0, tiled=True)  123 us
    reduce_scatter x1, waiting for transfers between devices, on_device(): lax.psum_scatter(weight_part, 'ctx', scatter_dimension=0, tiled=True)  90.6 us
    reduce_scatter x1, waiting for transfers between devices, on_device(): lax.psum_scatter(rope_grad, 'ctx', scatter_dimension=0, tiled=True)  86 us
    psum x1, waiting for transfers between devices, on_device(): d_latent, d_rope = lax.psum((lat_mine, rope_mine), 'head')  79.6 us
    all_gather x1, waiting for transfers between devices, on_device(): lax.all_gather(latent, 'ctx', axis=0, tiled=True)  60.3 us
    all_gather x1, waiting for transfers between devices, on_device(): lax.all_gather(rope_keys, 'ctx', axis=0, tiled=True)  47 us
    dot_general x16, matrix products, block_scores(): jnp.einsum('htr,kr->htk', query_lat, lat_piece, preferred_element_type=jn...  24.2 us
    dot_general x8, matrix products, grad_step(): jnp.einsum('htk,kr->htr', grad_scores, lat_piece, preferred_element_type=...  22.6 us
  transfers between devices with their start and end apart: 6, of which 6 were waited for; matrix products, arithmetic and copies ran while one was open for 1% of the time, Pallas kernels for 0%

commit v1 on v0

v1 whole, which is shorter than its diff:
```python
import math

import jax
import jax.numpy as jnp
from jax import lax
from jax.experimental import pallas as pl
from jax.experimental.pallas import tpu as pltpu
from jax.sharding import PartitionSpec as P

KVG = 8
NOPE = 112
ROPE = 16
HD = 128
TOK = 128
LH = 4
R = 512
AUG = 640
NQ = 4
NK = 8
ROWS = LH * TOK
KEYS = NK * TOK
F32 = jnp.float32
BF16 = jnp.bfloat16
NEG = -1e30
SCALE = 1.0 / math.sqrt(HD)
LOG2E = math.log2(math.e)
MESH = pl.DeviceIdType.MESH

Q_R, Q_L, Q_F, C_R, C_L, C_F, D_R, D_L, D_O = range(9)
LAT_Z, ROPE_Z, LAT_C, ROPE_C = 9, 12, 15, 19
STAT = 23
DL_C, DL_Y, DL_Z, DL_G = 26, 27, 30, 38
DQ_X = 46
DW_C, DW_X, DW_Z = 49, 50, 53
DR_C, DR_Z, DR_G = 56, 57, 60
N_COPY = 68


def nt(a, b):
    return lax.dot_general(a, b, (((1,), (1,)), ((), ())), preferred_element_type=F32)


def nn(a, b):
    return jnp.dot(a, b, preferred_element_type=F32)


def iota(shape, dim):
    return lax.broadcasted_iota(jnp.int32, shape, dim)


def kernel(
    bo, q_in, lat_in, rope_in, wuk, wuv, cot_in, att_in,
    dq_out, dlat_out, drope_out, dw_out,
    q_all, c_all, delta, kaug, kr, rope_t, lat_t, waug, waug_t,
    qa_t, q_lat, o_lat_t, o_lat, s_t, dots_t, gs_t, pr_t,
    lse, lse_r, m_loc,
    dl_own, dl_send, dl_rcv, y_f, y_send, y_rcv, z_f, z_send, z_rcv, ag,
    dqa, dq_send, dq_own, dq_rcv,
    dw_acc, dw_f, dw_send, dw_c, dw_xf, dw_xs, dw_xr, dw_zf, dw_zs, dw_zr,
    dr_send, dr_c, dr_f, dr_z, dr_g,
    ssem, rsem,
):
    ctx = lax.axis_index("ctx")
    head = lax.axis_index("head")
    c, x, zh = ctx % 2, (ctx // 2) % 4, ctx // 8
    y, zl = head % 4, head // 4
    z = zh * 2 + zl

    def dev(zz, xx, yy, cc):
        zz, xx, yy = zz % 8, xx % 4, yy % 4
        return (((zz // 2) * 4 + xx) * 2 + cc, (zz % 2) * 4 + yy)

    sib = dev(z, x, y, 1 - c)

    def copy(src, dst, sid, rid, target):
        return pltpu.make_async_remote_copy(
            src_ref=src, dst_ref=dst, send_sem=ssem.at[sid], recv_sem=rsem.at[rid],
            device_id=target, device_id_type=MESH,
        )

    barrier = pltpu.get_barrier_semaphore()
    peers = [sib]
    peers += [dev(z, x + d, y, c) for d in range(1, 4)]
    peers += [dev(z + d, x, y, c) for d in range(1, 8)]
    peers += [dev(z, x, y + d, c) for d in range(1, 4)]
    peers += [dev(zh * 2 + 1 - zl, x, y + d, c) for d in range(1, 4)]
    for p in peers:
        pl.semaphore_signal(barrier, inc=1, device_id=p, device_id_type=MESH)

    rope_t[...] = jnp.transpose(rope_in[...].astype(F32)).astype(BF16)
    ones = jnp.ones((8, HD), BF16)
    for h in range(LH):
        cols = slice(h * HD, (h + 1) * HD)
        prod = cot_in[:, cols].astype(F32) * att_in[:, cols].astype(F32)
        high = prod.astype(BF16)
        low = (prod - high.astype(F32)).astype(BF16)
        delta[0, :, h * TOK:(h + 1) * TOK] = nt(ones, high) + nt(ones, low)
    q_all[0] = q_in[...]
    c_all[0] = cot_in[...]
    kr[0] = rope_t[pl.ds(pl.multiple_of(head * ROPE, ROPE), ROPE), :]
    pl.semaphore_wait(barrier, len(peers))

    right, left, far = dev(z, x + 1, y, c), dev(z, x + 3, y, c), dev(z, x + 2, y, c)
    s = 2 * zl - 1
    near = 3 - 2 * zl
    z_to = [dev(z + s + 8, x, y, c), dev(z + 2 * s + 8, x, y, c), dev(z + 3 * s + 8, x, y, c)]
    z_slot = [near, near, 2]
    other = 1 - zl
    z_group = [other * 4 + y, head, other * 4 + y]
    rope_own = [rope_t.at[pl.ds(pl.multiple_of(g * ROPE, ROPE), ROPE), :] for g in z_group]
    lat_dst = lambda slot: kaug.at[slot, :, pl.ds(0, R)]
    lat_z = [copy(lat_in, lat_dst(z_slot[i]), LAT_Z + i, LAT_Z + z_slot[i] - 1, z_to[i]) for i in range(3)]
    rope_z = [copy(rope_own[i], kr.at[z_slot[i]], ROPE_Z + i, ROPE_Z + z_slot[i] - 1, z_to[i]) for i in range(3)]
    lat_own = copy(lat_in, lat_dst(4), LAT_C, LAT_C, sib)
    kr_own = copy(kr.at[0], kr.at[4], ROPE_C, ROPE_C, sib)
    q_r = copy(q_in, q_all.at[1], Q_R, Q_R, right)
    q_l = copy(q_in, q_all.at[3], Q_L, Q_L, left)
    c_r = copy(cot_in, c_all.at[1], C_R, C_R, right)
    c_l = copy(cot_in, c_all.at[3], C_L, C_L, left)
    d_r = copy(delta.at[0], delta.at[1], D_R, D_R, right)
    d_l = copy(delta.at[0], delta.at[3], D_L, D_L, left)
    d_o = copy(delta.at[0], delta.at[2], D_O, D_O, far)
    q_f = copy(q_all.at[1], q_all.at[2], Q_F, Q_F, right)
    c_f = copy(c_all.at[3], c_all.at[2], C_F, C_F, left)
    first = [q_r, c_l, q_l, c_r, lat_z[0], lat_z[1], lat_z[2], lat_own, kr_own] + rope_z + [d_r, d_l, d_o]
    for op in first:
        op.start()

    ei, ej = iota((LH * NOPE, LH * HD), 0), iota((LH * NOPE, LH * HD), 1)
    spread = ((ei == (ej // HD) * NOPE + ej % HD) & (ej % HD < NOPE)).astype(F32).astype(BF16)
    waug[0:R, :] = nn(wuk[...], spread).astype(BF16)
    si, sj = iota((AUG - R, LH * HD), 0), iota((AUG - R, LH * HD), 1)
    waug[R:AUG, :] = (si == sj % HD - NOPE).astype(F32).astype(BF16)
    fi, fj = iota((LH * HD, LH * NOPE), 0), iota((LH * HD, LH * NOPE), 1)
    spread_t = ((fj == (fi // HD) * NOPE + fi % HD) & (fi % HD < NOPE)).astype(F32).astype(BF16)
    waug_t[:, 0:R] = nt(spread_t, wuk[...]).astype(BF16)
    ti, tj = iota((LH * HD, AUG - R), 0), iota((LH * HD, AUG - R), 1)
    waug_t[:, R:AUG] = (tj == ti % HD - NOPE).astype(F32).astype(BF16)
    kaug[0, :, 0:R] = lat_in[...]

    def project(slot):
        for h in range(LH):
            cols = slice(h * HD, (h + 1) * HD)
            rows = slice(h * TOK, (h + 1) * TOK)
            qh = q_all[slot, :, cols]
            ch = c_all[slot, :, cols]
            qa_t[slot, :, rows] = nt(waug[:, cols], qh).astype(BF16)
            q_lat[slot, rows, :] = nt(qh, waug[0:R, cols]).astype(BF16)
            o_lat_t[slot, :, rows] = nt(wuv[:, cols], ch).astype(BF16)
            o_lat[slot, rows, :] = nt(ch, wuv[:, cols]).astype(BF16)

    def wait_lat(e):
        copy(lat_in, lat_dst(e), LAT_Z + e - 1, LAT_Z + e - 1, sib).wait_recv()
        copy(kr.at[0], kr.at[e], ROPE_Z + e - 1, ROPE_Z + e - 1, sib).wait_recv()
        a = copy(lat_dst(e), lat_dst(4 + e), LAT_C + e, LAT_C + e, sib)
        b = copy(kr.at[e], kr.at[4 + e], ROPE_C + e, ROPE_C + e, sib)
        a.start()
        b.start()
        return [a, b]

    project(0)
    q_r.wait_recv()
    q_f.start()
    c_l.wait_recv()
    c_f.start()
    forwards = wait_lat(1) + wait_lat(3)
    q_l.wait_recv()
    project_3_ready = c_l
    project(3)
    c_r.wait_recv()
    project(1)
    forwards += wait_lat(2)
    lat_own.wait_recv()
    kr_own.wait_recv()
    for op in forwards:
        op.wait_recv()

    def key_block(b, carry):
        r16 = kr[b]
        wide = jnp.concatenate([r16.astype(F32), jnp.zeros((AUG - R - ROPE, TOK), F32)], axis=0)
        kaug[b, :, R:AUG] = jnp.transpose(wide).astype(BF16)
        lat_t[0:R, pl.ds(pl.multiple_of(b * TOK, TOK), TOK)] = jnp.transpose(kaug[b, :, 0:R])
        lat_t[R:R + ROPE, pl.ds(pl.multiple_of(b * TOK, TOK), TOK)] = r16
        return carry

    lax.fori_loop(0, NK, key_block, 0)

    key_order = []
    for cr in range(2):
        for e in range(4):
            cc = c if cr == 0 else 1 - c
            key_order.append(bo[(((zh + 4 - e) % 4) * 4 + x) * 2 + cc])

    ki, qi = iota((TOK, ROWS), 0), iota((TOK, ROWS), 1)
    lag = ki - qi % TOK

    def lanes(slot):
        return pl.ds(pl.multiple_of(slot * ROWS, ROWS), ROWS)

    def scores(slot):
        keys = kaug[...].reshape(KEYS, AUG)
        s_t[:, lanes(slot)] = nn(keys, qa_t[slot])
        q_order = bo[(zh * 4 + (x + 4 - slot) % 4) * 2 + c]
        top = jnp.full((8, ROWS), NEG, F32)
        for b in range(NK):
            rows = slice(b * TOK, (b + 1) * TOK)
            allowed = lag <= (q_order - key_order[b]) * TOK
            v = jnp.where(allowed, s_t[rows, lanes(slot)] * (SCALE * LOG2E), NEG)
            s_t[rows, lanes(slot)] = v
            top = jnp.maximum(top, jnp.max(v.reshape(TOK // 8, 8, ROWS), axis=0))
        top = jnp.max(top, axis=0, keepdims=True)
        total = jnp.zeros((8, ROWS), F32)
        for b in range(NK):
            rows = slice(b * TOK, (b + 1) * TOK)
            e = jnp.exp2(s_t[rows, lanes(slot)] - top)
            total = total + jnp.sum(e.reshape(TOK // 8, 8, ROWS), axis=0)
        total = jnp.sum(total, axis=0, keepdims=True)
        return top + jnp.log2(total)

    lse[...] = jnp.zeros_like(lse)
    lse[0:1, :] = scores(0)
    lse[1:2, :] = scores(1)
    lse[3:4, :] = scores(3)
    q_f.wait_recv()
    c_f.wait_recv()
    project(2)
    lse[2:3, :] = scores(2)

    stats = [copy(lse, lse_r.at[d - 1], STAT + d - 1, STAT + d - 1, dev(z, x + d, y, c)) for d in range(1, 4)]
    for op in stats:
        op.start()

    d_r.wait_recv()
    d_l.wait_recv()
    d_o.wait_recv()

    def dots_step(slot, carry):
        keys = kaug[:, :, 0:R].reshape(KEYS, R)
        dots_t[:, lanes(slot)] = nn(keys, o_lat_t[slot]) - delta[slot, 0:1, :]
        return carry

    lax.fori_loop(0, NQ, dots_step, 0)
    for op in stats:
        op.wait_recv()
    for slot in range(NQ):
        parts = [lse[slot:slot + 1, :]]
        for d in range(1, 4):
            row = (slot - d) % 4
            parts.append(lse_r[d - 1, row:row + 1, :])
        top = jnp.maximum(jnp.maximum(parts[0], parts[1]), jnp.maximum(parts[2], parts[3]))
        total = sum(jnp.exp2(p - top) for p in parts)
        m_loc[slot] = jnp.broadcast_to(top + jnp.log2(total), (8, ROWS))

    def grad_step(slot, carry):
        log_total = m_loc[slot, 0:1, :]
        for b in range(NK):
            rows = slice(b * TOK, (b + 1) * TOK)
            w = jnp.exp2(s_t[rows, lanes(slot)] - log_total)
            pr_t[rows, lanes(slot)] = w.astype(BF16)
            gs_t[rows, lanes(slot)] = (w * dots_t[rows, lanes(slot)] * SCALE).astype(BF16)
        return carry

    lax.fori_loop(0, NQ, grad_step, 0)

    half = KEYS // 2

    def key_grad(rows):
        q = q_lat[...].reshape(NQ * ROWS, R)
        o = o_lat[...].reshape(NQ * ROWS, R)
        return nn(gs_t[rows, :], q) + nn(pr_t[rows, :], o)

    def rope_grad(rows):
        total = jnp.zeros((ROPE, half), F32)
        for slot in range(NQ):
            total = total + nt(qa_t[slot, R:R + ROPE, :], gs_t[rows, slot * ROWS:(slot + 1) * ROWS])
        return total

    hi_rows, lo_rows = slice(half, KEYS), slice(0, half)
    dl_send[...] = key_grad(hi_rows).astype(BF16)
    dl_c = copy(dl_send, dl_rcv, DL_C, DL_C, sib)
    dl_c.start()
    rg = rope_grad(hi_rows)
    for e in range(4):
        dr_send[e] = rg[:, e * TOK:(e + 1) * TOK]
    dr_cc = copy(dr_send, dr_c, DR_C, DR_C, sib)
    dr_cc.start()
    dl_own[...] = key_grad(lo_rows)
    rg = rope_grad(lo_rows)
    dl_c.wait_recv()
    for j in range(4):
        v = dl_own[:, j * 128:(j + 1) * 128] + dl_rcv[:, j * 128:(j + 1) * 128].astype(F32)
        y_f[j] = v
        y_send[j] = v.astype(BF16)
    dl_y = [copy(y_send.at[(y + d) % 4], y_rcv.at[d - 1], DL_Y + d - 1, DL_Y + d - 1, dev(z, x, y + d, c)) for d in range(1, 4)]
    for op in dl_y:
        op.start()
    dr_cc.wait_recv()
    for e in range(4):
        dr_f[e] = rg[:, e * TOK:(e + 1) * TOK] + dr_c[e]
    dr_zz = [copy(dr_f.at[e], dr_z.at[e - 1], DR_Z + e - 1, DR_Z + e - 1, dev(z + 8 - 2 * e, x, y, c)) for e in range(1, 4)]
    for op in dr_zz:
        op.start()

    dw_acc[...] = jnp.zeros_like(dw_acc)
    dqa[R + ROPE:AUG, :] = jnp.zeros((AUG - R - ROPE, ROWS), BF16)

    def query_grad(slot, keep):
        dqa[0:R + ROPE, :] = nn(lat_t[...], gs_t[:, lanes(slot)]).astype(BF16)
        for h in range(LH):
            cols = slice(h * HD, (h + 1) * HD)
            g = dqa[:, cols]
            dq = nn(waug_t[cols, :], g)
            if keep:
                dq_own[cols, :] = dq
            else:
                dq_send[slot, cols, :] = dq.astype(BF16)
            dw_acc[:, cols] += nn(g[0:R, :], q_all[slot, :, cols])

    dq_x = [copy(dq_send.at[d], dq_rcv.at[d - 1], DQ_X + d - 1, DQ_X + d - 1, dev(z, x + 4 - d, y, c)) for d in range(1, 4)]
    query_grad(2, False)
    dq_x[1].start()
    query_grad(1, False)
    dq_x[0].start()

    for op in dl_y:
        op.wait_recv()
    v = y_f[y]
    for d in range(3):
        v = v + y_rcv[d].astype(F32)
    for i in range(8):
        z_f[i] = v[i * 64:(i + 1) * 64, :]
        z_send[i] = v[i * 64:(i + 1) * 64, :].astype(BF16)
    dl_z = []
    dl_z_in = []
    for e in range(4):
        for t in range(2):
            if e == 0 and t == 1:
                continue
            tz = other if e == 0 else t
            k = e * 2 + t if e else 0
            dl_z.append(copy(
                z_send.at[e * 2 + tz], z_rcv.at[e * 2 + zl], DL_Z + k,
                DL_Z + (0 if e == 0 else e * 2 + zl), dev(2 * (zh + 4 - e) + tz, x, y, c)))
            if e:
                dl_z_in.append(copy(z_send.at[0], z_rcv.at[e * 2 + t], DL_Z + k, DL_Z + k, sib))
            else:
                dl_z_in.append(copy(z_send.at[0], z_rcv.at[other], DL_Z, DL_Z, sib))
    for op in dl_z:
        op.start()

    query_grad(3, False)
    dq_x[2].start()
    query_grad(0, True)

    for zz in range(4):
        for xx in range(4):
            for cc in range(2):
                r0 = ((zz * 4 + xx) * 2 + cc) * 16
                dw_f[cc, xx, zz] = dw_acc[r0:r0 + 16, :]
                dw_send[cc, xx, zz] = dw_acc[r0:r0 + 16, :].astype(BF16)
    dw_cc = copy(dw_send.at[1 - c], dw_c, DW_C, DW_C, sib)
    dw_cc.start()

    for op in dl_z_in:
        op.wait_recv()
    v = z_f[zl] + z_rcv[other].astype(F32)
    for i in range(2, 8):
        v = v + z_rcv[i].astype(F32)
    ag[head] = v

    def to_heads(buf, base):
        out, come = [], []
        for j in range(1, 8):
            to = (head + j) % 8
            src = (head + 8 - j) % 8
            target = dev(zh * 2 + to // 4, x, to % 4, c)
            out.append(copy(buf.at[head], buf.at[head], base + j, base + j, target))
            come.append(copy(buf.at[head], buf.at[src], base + j, base + j, target))
        for op in out:
            op.start()
        return out, come

    dl_out, dl_come = to_heads(ag, DL_G)

    for op in dr_zz:
        op.wait_recv()
    dr_g[head] = dr_f[0] + dr_z[0] + dr_z[1] + dr_z[2]
    dr_out, dr_come = to_heads(dr_g, DR_G)

    dw_cc.wait_recv()
    v = dw_f[c] + dw_c[...].astype(F32)
    dw_xf[...] = v
    dw_xs[...] = v.astype(BF16)
    dw_x = [copy(dw_xs.at[(x + d) % 4], dw_xr.at[d - 1], DW_X + d - 1, DW_X + d - 1, dev(z, x + d, y, c)) for d in range(1, 4)]
    for op in dw_x:
        op.start()

    for op in dq_x:
        op.wait_recv()
    v = dq_own[...]
    for d in range(3):
        v = v + dq_rcv[d].astype(F32)
    dq_out[...] = jnp.transpose(v).astype(BF16)

    for op in dw_x:
        op.wait_recv()
    v = dw_xf[x]
    for d in range(3):
        v = v + dw_xr[d].astype(F32)
    dw_zf[...] = v
    dw_zs[...] = v.astype(BF16)
    dw_z = [copy(dw_zs.at[(zh + d) % 4], dw_zr.at[d - 1], DW_Z + d - 1, DW_Z + d - 1, dev(z + 2 * d, x, y, c)) for d in range(1, 4)]
    for op in dw_z:
        op.start()

    for op in dl_come:
        op.wait_recv()
    for i in range(8):
        dlat_out[(i // 4) * 64:(i // 4) * 64 + 64, (i % 4) * 128:(i % 4) * 128 + 128] = ag[i]
    for op in dr_come:
        op.wait_recv()
    drope_out[...] = jnp.transpose(dr_g[...].reshape(KVG * ROPE, TOK))
    for op in dw_z:
        op.wait_recv()
    v = dw_zf[zh]
    for d in range(3):
        v = v + dw_zr[d].astype(F32)
    dw_out[...] = v

    sent = first + [q_f, c_f] + forwards + stats + [dl_c, dr_cc] + dl_y + dr_zz + dq_x
    sent += dl_z + [dw_cc] + dl_out + dr_out + dw_x + dw_z
    for op in sent:
        op.wait_send()


def on_device(block_order, queries, latent, rope_keys, w_uk, w_uv, cotangent, attn_out):
    vm = lambda shape, kind: pltpu.VMEM(shape, kind)
    scratch = [
        vm((NQ, TOK, LH * HD), BF16), vm((NQ, TOK, LH * HD), BF16), vm((NQ, 8, ROWS), F32),
        vm((NK, TOK, AUG), BF16), vm((NK, ROPE, TOK), BF16), vm((KVG * ROPE, TOK), BF16),
        vm((R + ROPE, KEYS), BF16), vm((AUG, LH * HD), BF16), vm((LH * HD, AUG), BF16),
        vm((NQ, AUG, ROWS), BF16), vm((NQ, ROWS, R), BF16), vm((NQ, R, ROWS), BF16), vm((NQ, ROWS, R), BF16),
        vm((KEYS, NQ * ROWS), F32), vm((KEYS, NQ * ROWS), F32),
        vm((KEYS, NQ * ROWS), BF16), vm((KEYS, NQ * ROWS), BF16),
        vm((8, ROWS), F32), vm((3, 8, ROWS), F32), vm((NQ, 8, ROWS), F32),
        vm((KEYS // 2, R), F32), vm((KEYS // 2, R), BF16), vm((KEYS // 2, R), BF16),
        vm((4, KEYS // 2, 128), F32), vm((4, KEYS // 2, 128), BF16), vm((3, KEYS // 2, 128), BF16),
        vm((8, 64, 128), F32), vm((8, 64, 128), BF16), vm((8, 64, 128), BF16), vm((8, 64, 128), F32),
        vm((AUG, ROWS), BF16), vm((NQ, LH * HD, TOK), BF16), vm((LH * HD, TOK), F32), vm((3, LH * HD, TOK), BF16),
        vm((R, LH * HD), F32), vm((2, 4, 4, 16, LH * HD), F32), vm((2, 4, 4, 16, LH * HD), BF16),
        vm((4, 4, 16, LH * HD), BF16), vm((4, 4, 16, LH * HD), F32), vm((4, 4, 16, LH * HD), BF16),
        vm((3, 4, 16, LH * HD), BF16), vm((4, 16, LH * HD), F32), vm((4, 16, LH * HD), BF16),
        vm((3, 16, LH * HD), BF16),
        vm((4, ROPE, TOK), F32), vm((4, ROPE, TOK), F32), vm((4, ROPE, TOK), F32),
        vm((3, ROPE, TOK), F32), vm((KVG, ROPE, TOK), F32),
        pltpu.SemaphoreType.DMA((N_COPY,)), pltpu.SemaphoreType.DMA((N_COPY,)),
    ]
    vmem = pl.BlockSpec(memory_space=pltpu.VMEM)
    dq, dlat, drope, dw = pl.pallas_call(
        kernel,
        out_shape=(
            jax.ShapeDtypeStruct((TOK, LH * HD), BF16),
            jax.ShapeDtypeStruct((TOK, R), F32),
            jax.ShapeDtypeStruct((TOK, KVG * ROPE), F32),
            jax.ShapeDtypeStruct((16, LH * HD), F32),
        ),
        in_specs=[pl.BlockSpec(memory_space=pltpu.SMEM)] + [vmem] * 7,
        out_specs=(vmem,) * 4,
        scratch_shapes=scratch,
        compiler_params=pltpu.CompilerParams(
            collective_id=0, has_side_effects=True, vmem_limit_bytes=60 * 1024 * 1024
        ),
        name="latent_attention_grad",
    )(block_order, queries, latent, rope_keys, w_uk, w_uv, cotangent, attn_out)
    dw = dw.reshape(16, LH, HD)[:, :, :NOPE].reshape(16, LH * NOPE)
    return dq, dlat, drope, dw


def solution(mesh):
    return jax.shard_map(
        on_device,
        mesh=mesh,
        in_specs=(
            P(),
            P("ctx", "head"),
            P("ctx", None),
            P("ctx", None),
            P(None, "head"),
            P(None, "head"),
            P("ctx", "head"),
            P("ctx", "head"),
        ),
        out_specs=(P("ctx", "head"), P("ctx", None), P("ctx", None), P("ctx", "head")),
        check_vma=False,
    )
```

time: 667 us -> 77.7 us (0.12)
  waiting for transfers between devices: 487 us -> 0 us
  matrix products: 95 us -> 0 us
  Pallas kernels: 0 us -> 70.3 us
  local copies, waits for them, and re-layouts: 52.3 us -> 6.59 us
  between operations: 14.9 us -> 0.65 us
  other arithmetic: 12.4 us -> 0 us
    reduce_scatter x3 -> x0, waiting for transfers between devices: 299 us -> none  [the longest x1 123 us: on_device(): lax.psum_scatter(lat_grad, 'ctx', scatter_dimension=0, tiled=True)]
    all_gather x2 -> x0, waiting for transfers between devices: 107 us -> none  [the longest x1 60.3 us: on_device(): lax.all_gather(latent, 'ctx', axis=0, tiled=True)]
    dot_general x108 -> x0, matrix products: 95 us -> none  [the longest x16 24.2 us: block_scores(): jnp.einsum('htr,kr->htk', query_lat, lat_piece, preferred_element_type=jn...]
    psum x1 -> x0, waiting for transfers between devices: 79.6 us -> none  [on_device(): d_latent, d_rope = lax.psum((lat_mine, rope_mine), 'head')]
    pallas_call x0 -> x1, Pallas kernels: none -> 70.3 us  [on_device(): pl.pallas_call(kernel, out_shape=(jax.ShapeDtypeStruct((TOK, LH * HD), BF...]
    dynamic_slice x16 -> x0, local copies, waits for them, and re-layouts: 14.7 us -> none  [the longest x8 7.37 us: stats_loop(): lax.dynamic_slice_in_dim(whole_rope, begin_row, span, 0)]
    dynamic_update_slice x16 -> x0, local copies, waits for them, and re-layouts: 14.3 us -> none  [grad_step(): lax.dynamic_update_slice_in_dim(rope_grad, rope_block, begin_row, 0)]
    reduce_sum x26 -> x0, other arithmetic: 9.51 us -> none  [the longest x17 8.01 us: lookup_order(): return jnp.sum(jnp.where(hits, block_order[None, :], 0), axis=1)]
  transfers between devices with their start and end apart: 6 -> 0, of which waited for: 6 -> 0; matrix products, arithmetic and copies ran while one was open for 1% -> 0% of each run, Pallas kernels for 0% -> 0%
where the time goes in v1:
time: 77.7 us; the launch traced here: 77.5 us
  Pallas kernels  70.3 us (90%)
  local copies, waits for them, and re-layouts  6.59 us (8%)
    pallas_call x1, Pallas kernels, on_device(): pl.pallas_call(kernel, out_shape=(jax.ShapeDtypeStruct((TOK, LH * HD), BF...  70.3 us
    unnamed x8, local copies, waits for them, and re-layouts  5.08 us

profile of v1, /device:TPU:32, one launch (start us, length us, event | category | flops | bytes accessed | tf_op | source)
XLA Modules:
  0.0 77.5 jit_solution(7439601300825466447)
XLA Ops:
  0.6 2.0 %copy.12.wuk = bf16[512,448]{1,0:T(8,128)(2,1)} copy(bf16[512,448]{0,1:T(8,128)(2,1)} %param.12) | data formatting | bytes 917504 | tf_op args[4]
  2.6 70.3 %latent_attention_grad.1 = (bf16[128,512]{1,0:T(8,128)(2,1)}, f32[128,512]{1,0:T(8,128)}, f32[128,128]{1,0:T(8,128)}, f32[16,512]{1,0:T(8,128)}) custom-call(s32[32]{0:T(128)} %bo.1, bf16[128,512]{1,0:T(8,128)(2,1)} %q_in.1, bf16[128,512]{1,0:T(8,128)(2,1)} %lat_in.1, bf16[128,128]{1,0:T(8,128)(2,1)} %rope_in.1, bf16[512,448]{1,0:T(8,128)(2,1)} %copy.12.wuk, ...), custom_call_target="tpu_custom_call" | custom-call | tf_op jit(solution)/shard_map/latent_attention_grad/pallas_call | solution.py:459
  72.9 0.0 copy-start
  72.9 0.8 %reshape.14 = f32[16,4,128]{2,1,0:T(4,128)S(1)} reshape(f32[16,512]{1,0:T(8,128)} %get-tuple-element.11) | data formatting | bytes 65536 | tf_op jit(solution)/shard_map/reshape | solution.py:475
  73.8 0.7 reshape.15
  74.5 1.6 %copy.16 = bf16[128,512]{1,0:T(8,128)(2,1)} copy(bf16[128,512]{1,0:T(8,128)(2,1)} %get-tuple-element.16) | data formatting | bytes 262144
  76.0 0.0 copy-done
  76.0 0.0 copy-start.1
  76.0 0.7 copy.17
  76.7 0.2 copy-done.1
  76.9 0.6 copy.18
Async XLA Ops:
  72.9 3.1 %copy-start = (f32[128,512]{1,0:T(8,128)S(1)}, f32[128,512]{1,0:T(8,128)}, u32[]{:S(2)}) copy-start(f32[128,512]{1,0:T(8,128)} %get-tuple-element.17) | copy-start | bytes 786436
  76.0 0.9 %copy-start.1 = (f32[128,128]{1,0:T(8,128)S(1)}, f32[128,128]{1,0:T(8,128)}, u32[]{:S(2)}) copy-start(f32[128,128]{1,0:T(8,128)} %get-tuple-element.18) | copy-start | bytes 196612

commit v2 on v1

v2 whole, which is shorter than its diff:
```python
import math

import jax
import jax.numpy as jnp
from jax import lax
from jax.experimental import pallas as pl
from jax.experimental.pallas import tpu as pltpu
from jax.sharding import PartitionSpec as P

KVG = 8
NOPE = 112
ROPE = 16
HD = 128
TOK = 128
LH = 4
R = 512
AUG = 640
NQ = 4
ROWS = LH * TOK
F32 = jnp.float32
BF16 = jnp.bfloat16
NEG = -1e30
SCALE = 1.0 / math.sqrt(HD)
LOG2E = math.log2(math.e)
MESH = pl.DeviceIdType.MESH

PLACE = (0, 1, 3, 2)
STEP = (0, 1, 3, 2)

N_COPY = 0


def numbers(n):
    global N_COPY
    N_COPY += n
    return N_COPY - n


Q_R, Q_L, Q_F, C_R, C_L, C_F, D_R, D_L, D_F = (numbers(1) for _ in range(9))
LAT_Z, ROPE_Z, LAT_C, ROPE_C = numbers(4), numbers(4), numbers(3), numbers(4)
QUART_Z, QUART_Y, QUART_C = numbers(1), numbers(4), numbers(4)
STAT = numbers(4)
DL_C, DL_Y, DL_Z, DL_G = numbers(2), numbers(8), numbers(8), numbers(8)
DQ_X = numbers(4)
DW_C, DW_X, DW_Z = numbers(1), numbers(4), numbers(4)
DR_C, DR_Z, DR_G = numbers(1), numbers(4), numbers(8)


def nt(a, b):
    return lax.dot_general(a, b, (((1,), (1,)), ((), ())), preferred_element_type=F32)


def nn(a, b):
    return jnp.dot(a, b, preferred_element_type=F32)


def iota(shape, dim):
    return lax.broadcasted_iota(jnp.int32, shape, dim)


def kernel(
    bo, q_in, lat_in, rope_in, wuk_in, wuv_in, cot_in, att_in,
    dq_out, dlat_out, drope_out, dw_out,
    rope_v, wuk, wuv, att,
    q_all, c_all, delta, kaug, kr, rope_t, lat_t, waug, waug_t,
    qa_t, q_lat, o_lat_t, o_lat, s_t, dots_t, gs_t, pr_t,
    lse_p, lse, lse_r, log_tot,
    dl_send, dl_rcv, y_f, y_send, y_rcv, z_f, z_send, z_rcv, ag,
    dqa, dq_send, dq_own, dq_rcv,
    dw_acc, dw_f, dw_send, dw_c, dw_xf, dw_xs, dw_xr, dw_zf, dw_zs, dw_zr,
    dr_send, dr_c, dr_f, dr_z, dr_g,
    lsem, ssem, rsem,
):
    ctx = lax.axis_index("ctx")
    head = lax.axis_index("head")
    c, x, zh = ctx % 2, (ctx // 2) % 4, ctx // 8
    y, zl = head % 4, head // 4
    z = zh * 2 + zl
    other = 1 - zl

    def dev(zz, xx, yy, cc):
        zz, xx, yy = zz % 8, xx % 4, yy % 4
        return (((zz // 2) * 4 + xx) * 2 + cc, (zz % 2) * 4 + yy)

    sib = dev(z, x, y, 1 - c)

    def copy(src, dst, sid, rid, target):
        return pltpu.make_async_remote_copy(
            src_ref=src, dst_ref=dst, send_sem=ssem.at[sid], recv_sem=rsem.at[rid],
            device_id=target, device_id_type=MESH,
        )

    def start(*ops):
        for op in ops:
            op.start()
            sent.append(op)

    def arrive(*ops):
        for op in ops:
            op.wait_recv()

    sent = []

    barrier = pltpu.get_barrier_semaphore()
    peers = [dev(2 * zh + other, x, y + d, c) for d in range(1, 4)]
    peers += [dev(z + d, x, y, c) for d in (4, 3, 5, 2, 6, 1, 7)]
    peers += [dev(z, x, y + d, c) for d in range(1, 4)]
    peers += [dev(z, x + d, y, c) for d in range(1, 4)]
    peers += [sib]

    def lat_at(cr, place, rows=None):
        if rows is None:
            return kaug.at[cr, place, :, pl.ds(0, R)]
        return kaug.at[cr, place, rows, pl.ds(0, R)]

    loads = [
        pltpu.make_async_copy(rope_in, rope_v, lsem.at[0]),
        pltpu.make_async_copy(lat_in, lat_at(0, 0), lsem.at[1]),
        pltpu.make_async_copy(q_in, q_all.at[0], lsem.at[2]),
        pltpu.make_async_copy(cot_in, c_all.at[0], lsem.at[3]),
        pltpu.make_async_copy(wuk_in, wuk, lsem.at[4]),
        pltpu.make_async_copy(wuv_in, wuv, lsem.at[5]),
        pltpu.make_async_copy(att_in, att, lsem.at[6]),
    ]
    for op in loads:
        op.start()
    for p in peers:
        pl.semaphore_signal(barrier, inc=1, device_id=p, device_id_type=MESH)

    loads[0].wait()
    rope_t[...] = jnp.transpose(rope_v[...].astype(F32)).astype(BF16)
    kr[0, 0] = rope_t[pl.ds(pl.multiple_of(head * ROPE, ROPE), ROPE), :]
    for op in loads[1:]:
        op.wait()
    ones = jnp.ones((8, HD), BF16)
    for h in range(LH):
        cols = slice(h * HD, (h + 1) * HD)
        prod = c_all[0, :, cols].astype(F32) * att[:, cols].astype(F32)
        high = prod.astype(BF16)
        low = (prod - high.astype(F32)).astype(BF16)
        delta[0, :, h * TOK:(h + 1) * TOK] = nt(ones, high) + nt(ones, low)

    fi, fj = iota((LH * HD, LH * NOPE), 0), iota((LH * HD, LH * NOPE), 1)
    spread = ((fj == (fi // HD) * NOPE + fi % HD) & (fi % HD < NOPE)).astype(F32).astype(BF16)
    waug_t[:, 0:R] = nn(spread, wuk[...]).astype(BF16)
    ti, tj = iota((LH * HD, AUG - R), 0), iota((LH * HD, AUG - R), 1)
    waug_t[:, R:AUG] = (tj == ti % HD - NOPE).astype(F32).astype(BF16)
    waug[...] = jnp.transpose(waug_t[...])

    def project(slot):
        for h in range(LH):
            cols = slice(h * HD, (h + 1) * HD)
            rows = slice(h * TOK, (h + 1) * TOK)
            qh = q_all[slot, :, cols]
            ch = c_all[slot, :, cols]
            qa_t[slot, :, rows] = nt(waug[:, cols], qh).astype(BF16)
            q_lat[slot, rows, :] = nn(qh, waug_t[cols, 0:R]).astype(BF16)
            o_lat_t[slot, :, rows] = nt(wuv[:, cols], ch).astype(BF16)
            o_lat[slot, rows, :] = nt(ch, wuv[:, cols]).astype(BF16)

    def prepare(cr, place):
        r16 = kr[cr, place]
        wide = jnp.concatenate([r16.astype(F32), jnp.zeros((AUG - R - ROPE, TOK), F32)], axis=0)
        kaug[cr, place, :, R:AUG] = jnp.transpose(wide).astype(BF16)
        cols = slice((cr * 4 + place) * TOK, (cr * 4 + place + 1) * TOK)
        lat_t[0:R, cols] = jnp.transpose(kaug[cr, place, :, 0:R])
        lat_t[R:R + ROPE, cols] = r16

    prepare(0, 0)
    pl.semaphore_wait(barrier, len(peers))

    right, left = dev(z, x + 1, y, c), dev(z, x + 3, y, c)
    s = 2 * zl - 1
    to_1, to_2, to_3 = (dev(z + i * s + 8, x, y, c) for i in (1, 2, 3))
    near = 2 - zl
    early, late = 1 + zl, 2 - zl

    def rope_of(group):
        return rope_t.at[pl.ds(pl.multiple_of(group * ROPE, ROPE), ROPE), :]

    def quarter(yy):
        return pl.ds(pl.multiple_of(yy * 32, 32), 32)

    q_r = copy(q_all.at[0], q_all.at[1], Q_R, Q_R, right)
    q_l = copy(q_all.at[0], q_all.at[3], Q_L, Q_L, left)
    c_r = copy(c_all.at[0], c_all.at[1], C_R, C_R, right)
    c_l = copy(c_all.at[0], c_all.at[3], C_L, C_L, left)
    d_r = copy(delta.at[0], delta.at[1], D_R, D_R, right)
    d_l = copy(delta.at[0], delta.at[3], D_L, D_L, left)
    q_f = copy(q_all.at[1], q_all.at[2], Q_F, Q_F, right)
    c_f = copy(c_all.at[3], c_all.at[2], C_F, C_F, left)
    d_f = copy(delta.at[1], delta.at[2], D_F, D_F, right)
    part = quarter(y)
    quart = copy(lat_at(0, 0, part), lat_at(0, 3, part), QUART_Z, QUART_Z, to_3)
    lat_1 = copy(lat_at(0, 0), lat_at(0, near), LAT_Z + 1, LAT_Z + near, to_1)
    lat_2 = copy(lat_at(0, 0), lat_at(0, near), LAT_Z + 2, LAT_Z + near, to_2)
    rope_1 = copy(rope_of(other * 4 + y), kr.at[0, near], ROPE_Z + 1, ROPE_Z + near, to_1)
    rope_2 = copy(rope_of(head), kr.at[0, near], ROPE_Z + 2, ROPE_Z + near, to_2)
    rope_3 = copy(rope_of(other * 4 + y), kr.at[0, 3], ROPE_Z + 3, ROPE_Z + 3, to_3)
    lat_c = copy(lat_at(0, 0), lat_at(1, 0), LAT_C, LAT_C, sib)
    rope_c = [copy(kr.at[0, i], kr.at[1, i], ROPE_C + i, ROPE_C + i, sib) for i in (0, 3)]
    start(q_r, c_l, quart, lat_1, q_l, c_r, lat_2, lat_c, rope_c[0], rope_3, rope_1, rope_2, d_r, d_l)

    def from_z(place):
        arrive(copy(lat_at(0, 0), lat_at(0, place), LAT_Z + place, LAT_Z + place, sib))
        arrive(copy(kr.at[0, 0], kr.at[0, place], ROPE_Z + place, ROPE_Z + place, sib))

    def to_core(place):
        start(copy(lat_at(0, place), lat_at(1, place), LAT_C + place, LAT_C + place, sib))
        start(copy(kr.at[0, place], kr.at[1, place], ROPE_C + place, ROPE_C + place, sib))

    def from_core(place):
        arrive(copy(lat_at(0, 0), lat_at(1, place), LAT_C + place, LAT_C + place, sib))
        arrive(copy(kr.at[0, 0], kr.at[1, place], ROPE_C + place, ROPE_C + place, sib))

    key_order = []
    for cr in range(2):
        for place in range(4):
            cc = c if cr == 0 else 1 - c
            key_order.append(bo[(((zh + 4 - STEP[place]) % 4) * 4 + x) * 2 + cc])
    lag = iota((TOK, ROWS), 0) - iota((TOK, ROWS), 1) % TOK

    def lanes(slot):
        return pl.ds(pl.multiple_of(slot * ROWS, ROWS), ROWS)

    def keys_of(a, b, width):
        return kaug[:, a:b, :, 0:width].reshape(2 * (b - a) * TOK, width)

    def scores(slot, a, b):
        v = nn(keys_of(a, b, AUG), qa_t[slot])
        q_order = bo[(zh * 4 + (x + 4 - slot) % 4) * 2 + c]
        top = jnp.full((8, ROWS), NEG, F32)
        for cr in range(2):
            for place in range(a, b):
                i = cr * (b - a) + place - a
                allowed = lag <= (q_order - key_order[cr * 4 + place]) * TOK
                w = jnp.where(allowed, v[i * TOK:(i + 1) * TOK, :] * (SCALE * LOG2E), NEG)
                s_t[cr, place, :, lanes(slot)] = w
                top = jnp.maximum(top, jnp.max(w.reshape(TOK // 8, 8, ROWS), axis=0))
        top = jnp.max(top, axis=0, keepdims=True)
        total = jnp.zeros((8, ROWS), F32)
        for cr in range(2):
            for place in range(a, b):
                e = jnp.exp2(s_t[cr, place, :, lanes(slot)] - top)
                total = total + jnp.sum(e.reshape(TOK // 8, 8, ROWS), axis=0)
        return top + jnp.log2(jnp.sum(total, axis=0, keepdims=True))

    def dots(slot, a, b):
        v = nn(keys_of(a, b, R), o_lat_t[slot]) - delta[slot, 0:1, :]
        dots_t[:, a:b, :, lanes(slot)] = v.reshape(2, b - a, TOK, ROWS)

    def both_step(group, a, b):
        def step(i, carry):
            slot = i + i // 2
            lse_p[slot, group:group + 1, :] = scores(slot, a, b)
            dots(slot, a, b)
            return carry

        return step

    project(0)
    from_core(0)
    prepare(1, 0)
    both_step(0, 0, 1)(0, 0)
    arrive(q_r)
    start(q_f)
    arrive(c_l)
    start(c_f)
    arrive(quart)
    quart_y = [copy(lat_at(0, 3, part), lat_at(0, 3, part), QUART_Y + d, QUART_Y + d, dev(z, x, y + d, c)) for d in range(1, 4)]
    quart_c = [copy(lat_at(0, 3, quarter((y + 4 - d) % 4)), lat_at(1, 3, quarter((y + 4 - d) % 4)), QUART_C + d, QUART_C + d, sib) for d in range(4)]
    start(*quart_y)
    start(quart_c[0])
    from_z(early)
    to_core(early)
    arrive(q_l)
    project(3)
    arrive(c_r)
    project(1)
    arrive(d_r)
    start(d_f)
    arrive(d_l)
    from_z(late)
    to_core(late)
    lax.fori_loop(1, 3, both_step(0, 0, 1), 0)
    for d in range(1, 4):
        src = quarter((y + 4 - d) % 4)
        arrive(copy(lat_at(0, 3, part), lat_at(0, 3, src), QUART_Y + d, QUART_Y + d, sib))
        start(quart_c[d])
    arrive(copy(kr.at[0, 0], kr.at[0, 3], ROPE_Z + 3, ROPE_Z + 3, sib))
    start(rope_c[1])
    from_core(1)
    from_core(2)
    for place in (1, 2):
        prepare(0, place)
        prepare(1, place)
    lax.fori_loop(0, 3, both_step(1, 1, 3), 0)
    arrive(*quart_c)
    arrive(rope_c[1])
    prepare(0, 3)
    prepare(1, 3)

    def last_step(i, carry):
        slot = i + i // 2
        parts = [scores(slot, 3, 4), lse_p[slot, 0:1, :], lse_p[slot, 1:2, :]]
        top = jnp.maximum(jnp.maximum(parts[0], parts[1]), parts[2])
        lse_p[slot, 2:3, :] = top + jnp.log2(sum(jnp.exp2(p - top) for p in parts))
        return carry

    lax.fori_loop(0, 3, last_step, 0)
    arrive(q_f)
    arrive(c_f)
    project(2)
    lse[...] = jnp.zeros_like(lse)
    lse[2:3, :] = scores(2, 0, 4)
    for slot in (0, 1, 3):
        lse[slot:slot + 1, :] = lse_p[slot, 2:3, :]

    stats = [copy(lse, lse_r.at[d - 1], STAT + d, STAT + d, dev(z, x + d, y, c)) for d in range(1, 4)]
    start(*stats)
    arrive(d_f)

    def dots_step(i, carry):
        dots(i + i // 2, 3, 4)
        return carry

    lax.fori_loop(0, 3, dots_step, 0)
    dots(2, 0, 4)
    arrive(*stats)
    for slot in range(NQ):
        parts = [lse[slot:slot + 1, :]]
        for d in range(1, 4):
            row = (slot - d) % 4
            parts.append(lse_r[d - 1, row:row + 1, :])
        top = jnp.maximum(jnp.maximum(parts[0], parts[1]), jnp.maximum(parts[2], parts[3]))
        total = sum(jnp.exp2(p - top) for p in parts)
        log_tot[slot] = jnp.broadcast_to(top + jnp.log2(total), (8, ROWS))

    def grad_step(slot, carry):
        log_total = log_tot[slot, 0:1, :]
        for cr in range(2):
            for place in range(4):
                w = jnp.exp2(s_t[cr, place, :, lanes(slot)] - log_total)
                pr_t[cr, place, :, lanes(slot)] = w.astype(BF16)
                gs_t[cr, place, :, lanes(slot)] = (w * dots_t[cr, place, :, lanes(slot)] * SCALE).astype(BF16)
        return carry

    lax.fori_loop(0, NQ, grad_step, 0)

    def key_grad(cr, chunk):
        q = q_lat[...].reshape(NQ * ROWS, R)
        o = o_lat[...].reshape(NQ * ROWS, R)
        g = gs_t[cr, 2 * chunk:2 * chunk + 2].reshape(2 * TOK, NQ * ROWS)
        p = pr_t[cr, 2 * chunk:2 * chunk + 2].reshape(2 * TOK, NQ * ROWS)
        return nn(g, q) + nn(p, o)

    def rope_grad(cr):
        total = jnp.zeros((ROPE, 4 * TOK), F32)
        for slot in range(NQ):
            g = gs_t[cr, :, :, slot * ROWS:(slot + 1) * ROWS].reshape(4 * TOK, ROWS)
            total = total + nt(qa_t[slot, R:R + ROPE, :], g)
        return total

    dl_c = [copy(dl_send.at[k], dl_rcv.at[k], DL_C + k, DL_C + k, sib) for k in range(2)]
    dr_cc = copy(dr_send, dr_c, DR_C, DR_C, sib)
    dl_y = []
    for k in range(2):
        dl_send[k] = key_grad(1, k).astype(BF16)
        start(dl_c[k])
        if k == 0:
            rg = rope_grad(1)
            for e in range(4):
                dr_send[e] = rg[:, e * TOK:(e + 1) * TOK]
            start(dr_cc)
        mine = key_grad(0, k)
        arrive(dl_c[k])
        for j in range(4):
            v = mine[:, j * 128:(j + 1) * 128] + dl_rcv[k, :, j * 128:(j + 1) * 128].astype(F32)
            y_f[k, j] = v
            y_send[k, j] = v.astype(BF16)
        ops = [copy(y_send.at[k, (y + d) % 4], y_rcv.at[k, d - 1], DL_Y + 4 * k + d, DL_Y + 4 * k + d, dev(z, x, y + d, c)) for d in (2, 1, 3)]
        start(*ops)
        dl_y.append(ops)

    rg = rope_grad(0)
    arrive(dr_cc)
    for e in range(4):
        dr_f[e] = rg[:, e * TOK:(e + 1) * TOK] + dr_c[e]
    dr_zz = [copy(dr_f.at[i], dr_z.at[i - 1], DR_Z + i, DR_Z + i, dev(z + 8 - 2 * STEP[i], x, y, c)) for i in range(1, 4)]
    start(*dr_zz)

    dw_acc[...] = jnp.zeros_like(dw_acc)
    dqa[R + ROPE:AUG, :] = jnp.zeros((AUG - R - ROPE, ROWS), BF16)

    def query_grad(slot, keep):
        g_all = gs_t[:, :, :, slot * ROWS:(slot + 1) * ROWS].reshape(8 * TOK, ROWS)
        dqa[0:R + ROPE, :] = nn(lat_t[...], g_all).astype(BF16)
        for h in range(LH):
            cols = slice(h * HD, (h + 1) * HD)
            g = dqa[:, cols]
            dq = nn(waug_t[cols, :], g)
            if keep:
                dq_own[cols, :] = dq
            else:
                dq_send[slot, cols, :] = dq.astype(BF16)
            dw_acc[:, cols] += nn(g[0:R, :], q_all[slot, :, cols])

    dq_x = [copy(dq_send.at[d], dq_rcv.at[d - 1], DQ_X + d, DQ_X + d, dev(z, x + 4 - d, y, c)) for d in range(1, 4)]

    dl_z_in = []

    def along_z(k):
        arrive(*dl_y[k])
        v = y_f[k, y]
        for d in range(3):
            v = v + y_rcv[k, d].astype(F32)
        for i in range(4):
            piece = v[i * 64:(i + 1) * 64, :]
            z_send[4 * k + i] = piece.astype(BF16)
            if k == 0 and i < 2:
                z_f[i] = piece
        for place in (2 * k, 2 * k + 1):
            e = STEP[place]
            for t in range(2):
                if e == 0 and t == 1:
                    continue
                tz = other if e == 0 else t
                start(copy(
                    z_send.at[place * 2 + tz], z_rcv.at[place * 2 + zl], DL_Z + place * 2 + t,
                    DL_Z + (0 if e == 0 else place * 2 + zl), dev(2 * (zh + 4 - e) + tz, x, y, c)))
                if e:
                    dl_z_in.append(copy(z_send.at[0], z_rcv.at[place * 2 + t], DL_Z + place * 2 + t, DL_Z + place * 2 + t, sib))
                else:
                    dl_z_in.append(copy(z_send.at[0], z_rcv.at[other], DL_Z, DL_Z, sib))

    query_grad(2, False)
    start(dq_x[1])
    query_grad(1, False)
    start(dq_x[0])
    along_z(0)
    query_grad(3, False)
    start(dq_x[2])
    query_grad(0, True)

    for zz in range(4):
        for xx in range(4):
            for cc in range(2):
                r0 = ((zz * 4 + xx) * 2 + cc) * 16
                dw_f[cc, xx, zz] = dw_acc[r0:r0 + 16, :]
                dw_send[cc, xx, zz] = dw_acc[r0:r0 + 16, :].astype(BF16)
    dw_cc = copy(dw_send.at[1 - c], dw_c, DW_C, DW_C, sib)
    start(dw_cc)
    along_z(1)

    def to_heads(buf, base):
        come = []
        for j in (6, 2, 5, 7, 1, 3, 4):
            to = (head + j) % 8
            src = (head + 8 - j) % 8
            target = dev(zh * 2 + to // 4, x, to % 4, c)
            start(copy(buf.at[head], buf.at[head], base + j, base + j, target))
            come.append(copy(buf.at[head], buf.at[src], base + j, base + j, target))
        return come

    arrive(dw_cc)
    v = dw_f[c] + dw_c[...].astype(F32)
    dw_xf[...] = v
    dw_xs[...] = v.astype(BF16)
    dw_x = [copy(dw_xs.at[(x + d) % 4], dw_xr.at[d - 1], DW_X + d, DW_X + d, dev(z, x + d, y, c)) for d in range(1, 4)]
    start(dw_x[1], dw_x[0], dw_x[2])

    arrive(*dr_zz)
    dr_g[head] = dr_f[0] + dr_z[0] + dr_z[1] + dr_z[2]
    dr_come = to_heads(dr_g, DR_G)

    arrive(*dq_x)
    v = dq_own[...]
    for d in range(3):
        v = v + dq_rcv[d].astype(F32)
    dq_out[...] = jnp.transpose(v).astype(BF16)

    arrive(*dl_z_in)
    v = z_f[zl] + z_rcv[other].astype(F32)
    for i in range(2, 8):
        v = v + z_rcv[i].astype(F32)
    ag[head] = v.astype(BF16)
    dl_come = to_heads(ag, DL_G)

    arrive(*dw_x)
    v = dw_xf[x]
    for d in range(3):
        v = v + dw_xr[d].astype(F32)
    dw_zf[...] = v
    dw_zs[...] = v.astype(BF16)
    dw_z = [copy(dw_zs.at[(zh + d) % 4], dw_zr.at[d - 1], DW_Z + d, DW_Z + d, dev(z + 2 * d, x, y, c)) for d in range(1, 4)]
    start(dw_z[1], dw_z[0], dw_z[2])

    arrive(*dr_come)
    drope_out[...] = dr_g[...]
    arrive(*dl_come)
    dlat_out[...] = ag[...]
    arrive(*dw_z)
    v = dw_zf[zh]
    for d in range(3):
        v = v + dw_zr[d].astype(F32)
    dw_out[...] = v

    for op in sent:
        op.wait_send()


def finish(dq_in, ag, dr_g, dw_in, dq_out, dlat_out, drope_out, dw_out):
    dq_out[...] = dq_in[...]
    for i in range(8):
        dlat_out[(i // 4) * 64:(i // 4) * 64 + 64, (i % 4) * 128:(i % 4) * 128 + 128] = ag[i].astype(F32)
    drope_out[...] = jnp.transpose(dr_g[...].reshape(KVG * ROPE, TOK))
    dw_out[...] = jnp.concatenate([dw_in[:, h * HD:h * HD + NOPE] for h in range(LH)], axis=1)


def on_device(block_order, queries, latent, rope_keys, w_uk, w_uv, cotangent, attn_out):
    vm = lambda shape, kind: pltpu.VMEM(shape, kind)
    wide = LH * HD
    scratch = [
        vm((TOK, KVG * ROPE), BF16), vm((LH * NOPE, R), BF16), vm((R, wide), BF16), vm((TOK, wide), BF16),
        vm((NQ, TOK, wide), BF16), vm((NQ, TOK, wide), BF16), vm((NQ, 8, ROWS), F32),
        vm((2, 4, TOK, AUG), BF16), vm((2, 4, ROPE, TOK), BF16), vm((KVG * ROPE, TOK), BF16),
        vm((R + ROPE, 8 * TOK), BF16), vm((AUG, wide), BF16), vm((wide, AUG), BF16),
        vm((NQ, AUG, ROWS), BF16), vm((NQ, ROWS, R), BF16), vm((NQ, R, ROWS), BF16), vm((NQ, ROWS, R), BF16),
        vm((2, 4, TOK, NQ * ROWS), F32), vm((2, 4, TOK, NQ * ROWS), F32),
        vm((2, 4, TOK, NQ * ROWS), BF16), vm((2, 4, TOK, NQ * ROWS), BF16),
        vm((NQ, 8, ROWS), F32), vm((8, ROWS), F32), vm((3, 8, ROWS), F32), vm((NQ, 8, ROWS), F32),
        vm((2, 2 * TOK, R), BF16), vm((2, 2 * TOK, R), BF16),
        vm((2, 4, 2 * TOK, 128), F32), vm((2, 4, 2 * TOK, 128), BF16), vm((2, 3, 2 * TOK, 128), BF16),
        vm((2, 64, 128), F32), vm((8, 64, 128), BF16), vm((8, 64, 128), BF16), vm((8, 64, 128), BF16),
        vm((AUG, ROWS), BF16), vm((NQ, wide, TOK), BF16), vm((wide, TOK), F32), vm((3, wide, TOK), BF16),
        vm((R, wide), F32), vm((2, 4, 4, 16, wide), F32), vm((2, 4, 4, 16, wide), BF16),
        vm((4, 4, 16, wide), BF16), vm((4, 4, 16, wide), F32), vm((4, 4, 16, wide), BF16),
        vm((3, 4, 16, wide), BF16), vm((4, 16, wide), F32), vm((4, 16, wide), BF16),
        vm((3, 16, wide), BF16),
        vm((4, ROPE, TOK), F32), vm((4, ROPE, TOK), F32), vm((4, ROPE, TOK), F32),
        vm((3, ROPE, TOK), F32), vm((KVG, ROPE, TOK), F32),
        pltpu.SemaphoreType.DMA((7,)), pltpu.SemaphoreType.DMA((N_COPY,)), pltpu.SemaphoreType.DMA((N_COPY,)),
    ]
    vmem = pl.BlockSpec(memory_space=pltpu.VMEM)
    anywhere = pl.BlockSpec(memory_space=pl.ANY)
    parts = pl.pallas_call(
        kernel,
        out_shape=(
            jax.ShapeDtypeStruct((TOK, wide), BF16),
            jax.ShapeDtypeStruct((8, 64, 128), BF16),
            jax.ShapeDtypeStruct((KVG, ROPE, TOK), F32),
            jax.ShapeDtypeStruct((16, wide), F32),
        ),
        in_specs=[pl.BlockSpec(memory_space=pltpu.SMEM)] + [anywhere] * 7,
        out_specs=(vmem,) * 4,
        scratch_shapes=scratch,
        compiler_params=pltpu.CompilerParams(
            collective_id=0, has_side_effects=True, vmem_limit_bytes=60 * 1024 * 1024
        ),
        name="latent_attention_grad",
    )(block_order, queries, latent, rope_keys, w_uk.T, w_uv, cotangent, attn_out)
    return pl.pallas_call(
        finish,
        out_shape=(
            jax.ShapeDtypeStruct((TOK, wide), BF16),
            jax.ShapeDtypeStruct((TOK, R), F32),
            jax.ShapeDtypeStruct((TOK, KVG * ROPE), F32),
            jax.ShapeDtypeStruct((16, LH * NOPE), F32),
        ),
        in_specs=[vmem] * 4,
        out_specs=(vmem,) * 4,
        name="finish",
    )(*parts)


def solution(mesh):
    return jax.shard_map(
        on_device,
        mesh=mesh,
        in_specs=(
            P(),
            P("ctx", "head"),
            P("ctx", None),
            P("ctx", None),
            P(None, "head"),
            P(None, "head"),
            P("ctx", "head"),
            P("ctx", "head"),
        ),
        out_specs=(P("ctx", "head"), P("ctx", None), P("ctx", None), P("ctx", "head")),
        check_vma=False,
    )
```

time: 77.7 us -> 61.8 us (0.80)
  Pallas kernels: 70.3 us -> 61 us
  local copies, waits for them, and re-layouts: 6.59 us -> 0 us
    pallas_call x1 -> x2, Pallas kernels: 70.3 us -> 61 us  [the longest x1 59.2 us: on_device(): pl.pallas_call(kernel, out_shape=(jax.ShapeDtypeStruct((TOK, wide), BF16)...]
    unnamed x8 -> x0, local copies, waits for them, and re-layouts: 5.08 us -> none
    reshape x2 -> x0, local copies, waits for them, and re-layouts: 1.51 us -> none  [on_device(): dw = dw.reshape(16, LH, HD)[:, :, :NOPE].reshape(16, LH * NOPE)]
where the time goes in v2:
time: 61.8 us; the launch traced here: 61.7 us
  Pallas kernels  61 us (99%)
  between operations  0.64 us (1%)
    pallas_call x1, Pallas kernels, on_device(): pl.pallas_call(kernel, out_shape=(jax.ShapeDtypeStruct((TOK, wide), BF16)...  59.2 us
    pallas_call x1, Pallas kernels, on_device(): pl.pallas_call(finish, out_shape=(jax.ShapeDtypeStruct((TOK, wide), BF16)...  1.8 us

profile of v2, /device:TPU:32, one launch (start us, length us, event | category | flops | bytes accessed | tf_op | source)
XLA Modules:
  0.0 61.7 jit_solution(4704821621290486161)
XLA Ops:
  0.6 59.2 %latent_attention_grad.1 = (bf16[128,512]{1,0:T(8,128)(2,1)}, bf16[8,64,128]{2,1,0:T(8,128)(2,1)}, f32[8,16,128]{2,1,0:T(8,128)}, f32[16,512]{1,0:T(8,128)}) custom-call(s32[32]{0:T(128)} %bo.1, bf16[128,512]{1,0:T(8,128)(2,1)} %q_in.1, bf16[128,512]{1,0:T(8,128)(2,1)} %lat_in.1, bf16[128,128]{1,0:T(8,128)(2,1)} %rope_in.1, bf16[448,512]{1,0:T(8,128)(2,1)} %bitcast.1, ...), custom_call_target="tpu_custom_call" | custom-call | tf_op jit(solution)/shard_map/latent_attention_grad/pallas_call | solution.py:546
  59.9 1.8 %finish.1 = (bf16[128,512]{1,0:T(8,128)(2,1)}, f32[128,512]{1,0:T(8,128)}, f32[128,128]{1,0:T(8,128)}, f32[16,448]{1,0:T(8,128)}) custom-call(bf16[128,512]{1,0:T(8,128)(2,1)} %get-tuple-element.8.dq_in, bf16[8,64,128]{2,1,0:T(8,128)(2,1)} %get-tuple-element.9.ag, f32[8,16,128]{2,1,0:T(8,128)} %get-tuple-element.10.dr_g, f32[16,512]{1,0:T(8,128)} %get-tuple-element.11.dw_in), custom_call_target="tpu_custom_call" | custom-call | tf_op jit(solution)/shard_map/finish/pallas_call | solution.py:562

commit v3 on v2

--- a/solution.py
+++ b/solution.py
@@ -36,11 +36,13 @@
     return N_COPY - n
 
 
-Q_R, Q_L, Q_F, C_R, C_L, C_F, D_R, D_L, D_F = (numbers(1) for _ in range(9))
+Q_R, Q_L, C_R, C_L, D_R, D_L, D_F = (numbers(1) for _ in range(7))
+Q_FR, Q_FL, C_FR, C_FL = (numbers(1) for _ in range(4))
 LAT_Z, ROPE_Z, LAT_C, ROPE_C = numbers(4), numbers(4), numbers(3), numbers(4)
 QUART_Z, QUART_Y, QUART_C = numbers(1), numbers(4), numbers(4)
 STAT = numbers(4)
 DL_C, DL_Y, DL_Z, DL_G = numbers(2), numbers(8), numbers(8), numbers(8)
+DL_W, DL_FAR = numbers(8), numbers(1)
 DQ_X = numbers(4)
 DW_C, DW_X, DW_Z = numbers(1), numbers(4), numbers(4)
 DR_C, DR_Z, DR_G = numbers(1), numbers(4), numbers(8)
@@ -65,9 +67,9 @@
     q_all, c_all, delta, kaug, kr, rope_t, lat_t, waug, waug_t,
     qa_t, q_lat, o_lat_t, o_lat, s_t, dots_t, gs_t, pr_t,
     lse_p, lse, lse_r, log_tot,
-    dl_send, dl_rcv, y_f, y_send, y_rcv, z_f, z_send, z_rcv, ag,
+    dl_send, dl_rcv, y_f, y_send, y_rcv, z_f, z_send, z_rcv, w_rcv, far_send, far_rcv, ag,
     dqa, dq_send, dq_own, dq_rcv,
-    dw_acc, dw_f, dw_send, dw_c, dw_xf, dw_xs, dw_xr, dw_zf, dw_zs, dw_zr,
+    dw_f, dw_send, dw_c, dw_xf, dw_xs, dw_xr, dw_zf, dw_zs, dw_zr,
     dr_send, dr_c, dr_f, dr_z, dr_g,
     lsem, ssem, rsem,
 ):
@@ -147,22 +149,25 @@
     waug_t[:, R:AUG] = (tj == ti % HD - NOPE).astype(F32).astype(BF16)
     waug[...] = jnp.transpose(waug_t[...])
 
-    def project(slot):
+    def project_scores(slot):
+        for h in range(LH):
+            cols = slice(h * HD, (h + 1) * HD)
+            qa_t[slot, :, h * TOK:(h + 1) * TOK] = nt(waug[:, cols], q_all[slot, :, cols]).astype(BF16)
+
+    def project_rest(slot):
         for h in range(LH):
             cols = slice(h * HD, (h + 1) * HD)
             rows = slice(h * TOK, (h + 1) * TOK)
-            qh = q_all[slot, :, cols]
             ch = c_all[slot, :, cols]
-            qa_t[slot, :, rows] = nt(waug[:, cols], qh).astype(BF16)
-            q_lat[slot, rows, :] = nn(qh, waug_t[cols, 0:R]).astype(BF16)
             o_lat_t[slot, :, rows] = nt(wuv[:, cols], ch).astype(BF16)
             o_lat[slot, rows, :] = nt(ch, wuv[:, cols]).astype(BF16)
+            q_lat[slot, rows, :] = nn(q_all[slot, :, cols], waug_t[cols, 0:R]).astype(BF16)
 
     def prepare(cr, place):
         r16 = kr[cr, place]
         wide = jnp.concatenate([r16.astype(F32), jnp.zeros((AUG - R - ROPE, TOK), F32)], axis=0)
         kaug[cr, place, :, R:AUG] = jnp.transpose(wide).astype(BF16)
-        cols = slice((cr * 4 + place) * TOK, (cr * 4 + place + 1) * TOK)
+        cols = pl.ds(pl.multiple_of((cr * 4 + place) * TOK, TOK), TOK)
         lat_t[0:R, cols] = jnp.transpose(kaug[cr, place, :, 0:R])
         lat_t[R:R + ROPE, cols] = r16
 
@@ -187,8 +192,11 @@
     c_l = copy(c_all.at[0], c_all.at[3], C_L, C_L, left)
     d_r = copy(delta.at[0], delta.at[1], D_R, D_R, right)
     d_l = copy(delta.at[0], delta.at[3], D_L, D_L, left)
-    q_f = copy(q_all.at[1], q_all.at[2], Q_F, Q_F, right)
-    c_f = copy(c_all.at[3], c_all.at[2], C_F, C_F, left)
+    lo, hi = pl.ds(0, 2 * HD), pl.ds(2 * HD, 2 * HD)
+    q_fr = copy(q_all.at[1, :, lo], q_all.at[2, :, lo], Q_FR, Q_FR, right)
+    q_fl = copy(q_all.at[3, :, hi], q_all.at[2, :, hi], Q_FL, Q_FL, left)
+    c_fr = copy(c_all.at[1, :, lo], c_all.at[2, :, lo], C_FR, C_FR, right)
+    c_fl = copy(c_all.at[3, :, hi], c_all.at[2, :, hi], C_FL, C_FL, left)
     d_f = copy(delta.at[1], delta.at[2], D_F, D_F, right)
     part = quarter(y)
     quart = copy(lat_at(0, 0, part), lat_at(0, 3, part), QUART_Z, QUART_Z, to_3)
@@ -199,7 +207,7 @@
     rope_3 = copy(rope_of(other * 4 + y), kr.at[0, 3], ROPE_Z + 3, ROPE_Z + 3, to_3)
     lat_c = copy(lat_at(0, 0), lat_at(1, 0), LAT_C, LAT_C, sib)
     rope_c = [copy(kr.at[0, i], kr.at[1, i], ROPE_C + i, ROPE_C + i, sib) for i in (0, 3)]
-    start(q_r, c_l, quart, lat_1, q_l, c_r, lat_2, lat_c, rope_c[0], rope_3, rope_1, rope_2, d_r, d_l)
+    start(q_r, q_l, quart, lat_1, lat_c, rope_c[0], lat_2, c_r, c_l, rope_1, rope_3, rope_2, d_r, d_l)
 
     def from_z(place):
         arrive(copy(lat_at(0, 0), lat_at(0, place), LAT_Z + place, LAT_Z + place, sib))
@@ -213,59 +221,54 @@
         arrive(copy(lat_at(0, 0), lat_at(1, place), LAT_C + place, LAT_C + place, sib))
         arrive(copy(kr.at[0, 0], kr.at[1, place], ROPE_C + place, ROPE_C + place, sib))
 
-    key_order = []
-    for cr in range(2):
-        for place in range(4):
-            cc = c if cr == 0 else 1 - c
-            key_order.append(bo[(((zh + 4 - STEP[place]) % 4) * 4 + x) * 2 + cc])
+    def key_order(cr, place):
+        step = place + (place // 2) * (1 - 2 * (place % 2))
+        cc = c + cr - 2 * c * cr
+        return bo[(((zh + 4 - step) % 4) * 4 + x) * 2 + cc]
+
     lag = iota((TOK, ROWS), 0) - iota((TOK, ROWS), 1) % TOK
 
     def lanes(slot):
         return pl.ds(pl.multiple_of(slot * ROWS, ROWS), ROWS)
 
-    def keys_of(a, b, width):
-        return kaug[:, a:b, :, 0:width].reshape(2 * (b - a) * TOK, width)
-
-    def scores(slot, a, b):
-        v = nn(keys_of(a, b, AUG), qa_t[slot])
+    def scores(slot, place):
+        v = nn(kaug[:, place].reshape(2 * TOK, AUG), qa_t[slot])
         q_order = bo[(zh * 4 + (x + 4 - slot) % 4) * 2 + c]
         top = jnp.full((8, ROWS), NEG, F32)
+        tiles = []
         for cr in range(2):
-            for place in range(a, b):
-                i = cr * (b - a) + place - a
-                allowed = lag <= (q_order - key_order[cr * 4 + place]) * TOK
-                w = jnp.where(allowed, v[i * TOK:(i + 1) * TOK, :] * (SCALE * LOG2E), NEG)
-                s_t[cr, place, :, lanes(slot)] = w
-                top = jnp.maximum(top, jnp.max(w.reshape(TOK // 8, 8, ROWS), axis=0))
+            allowed = lag <= (q_order - key_order(cr, place)) * TOK
+            w = jnp.where(allowed, v[cr * TOK:(cr + 1) * TOK, :] * (SCALE * LOG2E), NEG)
+            s_t[cr, place, :, lanes(slot)] = w
+            tiles.append(w)
+            top = jnp.maximum(top, jnp.max(w.reshape(TOK // 8, 8, ROWS), axis=0))
         top = jnp.max(top, axis=0, keepdims=True)
         total = jnp.zeros((8, ROWS), F32)
-        for cr in range(2):
-            for place in range(a, b):
-                e = jnp.exp2(s_t[cr, place, :, lanes(slot)] - top)
-                total = total + jnp.sum(e.reshape(TOK // 8, 8, ROWS), axis=0)
-        return top + jnp.log2(jnp.sum(total, axis=0, keepdims=True))
-
-    def dots(slot, a, b):
-        v = nn(keys_of(a, b, R), o_lat_t[slot]) - delta[slot, 0:1, :]
-        dots_t[:, a:b, :, lanes(slot)] = v.reshape(2, b - a, TOK, ROWS)
-
-    def both_step(group, a, b):
+        for w in tiles:
+            e = jnp.exp2(w - top)
+            total = total + jnp.sum(e.reshape(TOK // 8, 8, ROWS), axis=0)
+        part = top + jnp.log2(jnp.sum(total, axis=0, keepdims=True))
+        lse_p[place, slot] = jnp.broadcast_to(part, (8, ROWS))
+
+    def loop(n, slot_of, place):
         def step(i, carry):
-            slot = i + i // 2
-            lse_p[slot, group:group + 1, :] = scores(slot, a, b)
-            dots(slot, a, b)
+            scores(slot_of(i), place)
             return carry
 
-        return step
-
-    project(0)
+        lax.fori_loop(0, n, step, 0)
+
+    def odd(i):
+        return 1 + 2 * i
+
+    project_scores(0)
+    project_rest(0)
     from_core(0)
     prepare(1, 0)
-    both_step(0, 0, 1)(0, 0)
+    scores(0, 0)
     arrive(q_r)
-    start(q_f)
-    arrive(c_l)
-    start(c_f)
+    start(q_fr)
+    arrive(q_l)
+    start(q_fl)
     arrive(quart)
     quart_y = [copy(lat_at(0, 3, part), lat_at(0, 3, part), QUART_Y + d, QUART_Y + d, dev(z, x, y + d, c)) for d in range(1, 4)]
     quart_c = [copy(lat_at(0, 3, quarter((y + 4 - d) % 4)), lat_at(1, 3, quarter((y + 4 - d) % 4)), QUART_C + d, QUART_C + d, sib) for d in range(4)]
@@ -273,68 +276,70 @@
     start(quart_c[0])
     from_z(early)
     to_core(early)
-    arrive(q_l)
-    project(3)
+    project_scores(1)
+    project_scores(3)
+    prepare(0, early)
+    loop(2, odd, 0)
     arrive(c_r)
-    project(1)
+    start(c_fr)
+    arrive(c_l)
+    start(c_fl)
     arrive(d_r)
     start(d_f)
-    arrive(d_l)
+    from_core(early)
+    prepare(1, early)
+    scores(0, early)
     from_z(late)
     to_core(late)
-    lax.fori_loop(1, 3, both_step(0, 0, 1), 0)
+    loop(2, odd, early)
     for d in range(1, 4):
         src = quarter((y + 4 - d) % 4)
         arrive(copy(lat_at(0, 3, part), lat_at(0, 3, src), QUART_Y + d, QUART_Y + d, sib))
         start(quart_c[d])
     arrive(copy(kr.at[0, 0], kr.at[0, 3], ROPE_Z + 3, ROPE_Z + 3, sib))
     start(rope_c[1])
-    from_core(1)
-    from_core(2)
-    for place in (1, 2):
-        prepare(0, place)
-        prepare(1, place)
-    lax.fori_loop(0, 3, both_step(1, 1, 3), 0)
+    arrive(q_fr, q_fl)
+    project_scores(2)
+    prepare(0, late)
+    prepare(0, 3)
+    scores(2, 0)
+    scores(2, early)
+    from_core(late)
+    prepare(1, late)
+    loop(4, lambda i: i, late)
     arrive(*quart_c)
     arrive(rope_c[1])
-    prepare(0, 3)
     prepare(1, 3)
-
-    def last_step(i, carry):
-        slot = i + i // 2
-        parts = [scores(slot, 3, 4), lse_p[slot, 0:1, :], lse_p[slot, 1:2, :]]
-        top = jnp.maximum(jnp.maximum(parts[0], parts[1]), parts[2])
-        lse_p[slot, 2:3, :] = top + jnp.log2(sum(jnp.exp2(p - top) for p in parts))
+    loop(4, lambda i: i, 3)
+
+    def join(parts):
+        top = jnp.maximum(jnp.maximum(parts[0], parts[1]), jnp.maximum(parts[2], parts[3]))
+        return top + jnp.log2(sum(jnp.exp2(p - top) for p in parts))
+
+    lse[...] = jnp.zeros_like(lse)
+    for slot in range(NQ):
+        lse[slot:slot + 1, :] = join([lse_p[place, slot, 0:1, :] for place in range(4)])
+
+    stats = [copy(lse, lse_r.at[d - 1], STAT + d, STAT + d, dev(z, x + d, y, c)) for d in range(1, 4)]
+    start(stats[1], stats[0], stats[2])
+    project_rest(1)
+    project_rest(3)
+    arrive(d_l, d_f, c_fr, c_fl)
+    project_rest(2)
+
+    def dots_step(slot, carry):
+        v = nn(kaug[:, :, :, 0:R].reshape(8 * TOK, R), o_lat_t[slot]) - delta[slot, 0:1, :]
+        dots_t[:, :, :, lanes(slot)] = v.reshape(2, 4, TOK, ROWS)
         return carry
 
-    lax.fori_loop(0, 3, last_step, 0)
-    arrive(q_f)
-    arrive(c_f)
-    project(2)
-    lse[...] = jnp.zeros_like(lse)
-    lse[2:3, :] = scores(2, 0, 4)
-    for slot in (0, 1, 3):
-        lse[slot:slot + 1, :] = lse_p[slot, 2:3, :]
-
-    stats = [copy(lse, lse_r.at[d - 1], STAT + d, STAT + d, dev(z, x + d, y, c)) for d in range(1, 4)]
-    start(*stats)
-    arrive(d_f)
-
-    def dots_step(i, carry):
-        dots(i + i // 2, 3, 4)
-        return carry
-
-    lax.fori_loop(0, 3, dots_step, 0)
-    dots(2, 0, 4)
+    lax.fori_loop(0, NQ, dots_step, 0)
     arrive(*stats)
     for slot in range(NQ):
         parts = [lse[slot:slot + 1, :]]
         for d in range(1, 4):
             row = (slot - d) % 4
             parts.append(lse_r[d - 1, row:row + 1, :])
-        top = jnp.maximum(jnp.maximum(parts[0], parts[1]), jnp.maximum(parts[2], parts[3]))
-        total = sum(jnp.exp2(p - top) for p in parts)
-        log_tot[slot] = jnp.broadcast_to(top + jnp.log2(total), (8, ROWS))
+        log_tot[slot] = jnp.broadcast_to(join(parts), (8, ROWS))
 
     def grad_step(slot, carry):
         log_total = log_tot[slot, 0:1, :]
@@ -364,23 +369,98 @@
     dl_c = [copy(dl_send.at[k], dl_rcv.at[k], DL_C + k, DL_C + k, sib) for k in range(2)]
     dr_cc = copy(dr_send, dr_c, DR_C, DR_C, sib)
     dl_y = []
+    dl_w_in = []
+    far_y = (y + 2) % 4
+
+    def to_owners(k, piece, landing, base):
+        come = []
+        for place in (2 * k, 2 * k + 1):
+            e = STEP[place]
+            for t in range(2):
+                if e == 0 and t == 1:
+                    continue
+                tz = other if e == 0 else t
+                i = (place % 2) * 2
+                start(copy(
+                    piece(i + tz), landing.at[place * 2 + zl], base + place * 2 + t,
+                    base + (0 if e == 0 else place * 2 + zl), dev(2 * (zh + 4 - e) + tz, x, y, c)))
+                at = base + place * 2 + t
+                come.append(copy(z_send.at[0], landing.at[place * 2 + t if e else other], at, at, sib))
+        return come
+
     for k in range(2):
         dl_send[k] = key_grad(1, k).astype(BF16)
         start(dl_c[k])
-        if k == 0:
+        mine = key_grad(0, k)
+        if k == 1:
             rg = rope_grad(1)
             for e in range(4):
                 dr_send[e] = rg[:, e * TOK:(e + 1) * TOK]
             start(dr_cc)
-        mine = key_grad(0, k)
         arrive(dl_c[k])
         for j in range(4):
             v = mine[:, j * 128:(j + 1) * 128] + dl_rcv[k, :, j * 128:(j + 1) * 128].astype(F32)
             y_f[k, j] = v
             y_send[k, j] = v.astype(BF16)
-        ops = [copy(y_send.at[k, (y + d) % 4], y_rcv.at[k, d - 1], DL_Y + 4 * k + d, DL_Y + 4 * k + d, dev(z, x, y + d, c)) for d in (2, 1, 3)]
+        ops = [copy(y_send.at[k, (y + d) % 4], y_rcv.at[k, d // 2], DL_Y + 4 * k + d, DL_Y + 4 * k + d, dev(z, x, y + d, c)) for d in (1, 3)]
         start(*ops)
         dl_y.append(ops)
+        dl_w_in.extend(to_owners(k, lambda i: y_send.at[k, far_y, pl.ds(i * 64, 64)], w_rcv, DL_W))
+
+    for h in range(LH):
+        dqa[h, R + ROPE:AUG, :] = jnp.zeros((AUG - R - ROPE, NQ * TOK), BF16)
+
+    def latent_step(slot, carry):
+        g = nn(lat_t[...], gs_t[:, :, :, lanes(slot)].reshape(8 * TOK, ROWS)).astype(BF16)
+        for h in range(LH):
+            dqa[h, 0:R + ROPE, pl.ds(pl.multiple_of(slot * TOK, TOK), TOK)] = g[:, h * TOK:(h + 1) * TOK]
+        return carry
+
+    dq_x = [copy(dq_send.at[d], dq_rcv.at[d - 1], DQ_X + d, DQ_X + d, dev(z, x + 4 - d, y, c)) for d in range(1, 4)]
+
+    dl_z_in = []
+
+    def along_z(k):
+        arrive(*dl_y[k])
+        v = y_f[k, y]
+        for d in range(2):
+            v = v + y_rcv[k, d].astype(F32)
+        for i in range(4):
+            piece = v[i * 64:(i + 1) * 64, :]
+            z_send[4 * k + i] = piece.astype(BF16)
+            if k == 0 and i < 2:
+                z_f[i] = piece
+        dl_z_in.extend(to_owners(k, lambda i: z_send.at[4 * k + i], z_rcv, DL_Z))
+
+    lax.fori_loop(0, 3, latent_step, 0)
+    along_z(0)
+    lax.fori_loop(3, NQ, latent_step, 0)
+
+    for h in range(LH):
+        cols = slice(h * HD, (h + 1) * HD)
+        v = nn(dqa[h, 0:R, :], q_all[:, :, cols].reshape(NQ * TOK, HD))
+        for zz in range(4):
+            for xx in range(4):
+                for cc in range(2):
+                    r0 = ((zz * 4 + xx) * 2 + cc) * 16
+                    dw_f[cc, xx, zz, :, cols] = v[r0:r0 + 16, :]
+                    dw_send[cc, xx, zz, :, cols] = v[r0:r0 + 16, :].astype(BF16)
+    dw_cc = copy(dw_send.at[1 - c], dw_c, DW_C, DW_C, sib)
+    start(dw_cc)
+    for h in range(LH):
+        cols = slice(h * HD, (h + 1) * HD)
+        v = nn(waug_t[cols, :], dqa[h])
+        dq_own[cols, :] = v[:, 0:TOK]
+        for slot in range(1, NQ):
+            dq_send[slot, cols, :] = v[:, slot * TOK:(slot + 1) * TOK].astype(BF16)
+    along_z(1)
+    arrive(dw_cc)
+    v = dw_f[c] + dw_c[...].astype(F32)
+    dw_xf[...] = v
+    dw_xs[...] = v.astype(BF16)
+    dw_x = [copy(dw_xs.at[(x + d) % 4], dw_xr.at[d - 1], DW_X + d, DW_X + d, dev(z, x + d, y, c)) for d in range(1, 4)]
+    start(dw_x[1], dw_x[0], dw_x[2])
+    start(dq_x[1], dq_x[0], dq_x[2])
 
     rg = rope_grad(0)
     arrive(dr_cc)
@@ -389,68 +469,13 @@
     dr_zz = [copy(dr_f.at[i], dr_z.at[i - 1], DR_Z + i, DR_Z + i, dev(z + 8 - 2 * STEP[i], x, y, c)) for i in range(1, 4)]
     start(*dr_zz)
 
-    dw_acc[...] = jnp.zeros_like(dw_acc)
-    dqa[R + ROPE:AUG, :] = jnp.zeros((AUG - R - ROPE, ROWS), BF16)
-
-    def query_grad(slot, keep):
-        g_all = gs_t[:, :, :, slot * ROWS:(slot + 1) * ROWS].reshape(8 * TOK, ROWS)
-        dqa[0:R + ROPE, :] = nn(lat_t[...], g_all).astype(BF16)
-        for h in range(LH):
-            cols = slice(h * HD, (h + 1) * HD)
-            g = dqa[:, cols]
-            dq = nn(waug_t[cols, :], g)
-            if keep:
-                dq_own[cols, :] = dq
-            else:
-                dq_send[slot, cols, :] = dq.astype(BF16)
-            dw_acc[:, cols] += nn(g[0:R, :], q_all[slot, :, cols])
-
-    dq_x = [copy(dq_send.at[d], dq_rcv.at[d - 1], DQ_X + d, DQ_X + d, dev(z, x + 4 - d, y, c)) for d in range(1, 4)]
-
-    dl_z_in = []
-
-    def along_z(k):
-        arrive(*dl_y[k])
-        v = y_f[k, y]
-        for d in range(3):
-            v = v + y_rcv[k, d].astype(F32)
-        for i in range(4):
-            piece = v[i * 64:(i + 1) * 64, :]
-            z_send[4 * k + i] = piece.astype(BF16)
-            if k == 0 and i < 2:
-                z_f[i] = piece
-        for place in (2 * k, 2 * k + 1):
-            e = STEP[place]
-            for t in range(2):
-                if e == 0 and t == 1:
-                    continue
-                tz = other if e == 0 else t
-                start(copy(
-                    z_send.at[place * 2 + tz], z_rcv.at[place * 2 + zl], DL_Z + place * 2 + t,
-                    DL_Z + (0 if e == 0 else place * 2 + zl), dev(2 * (zh + 4 - e) + tz, x, y, c)))
-                if e:
-                    dl_z_in.append(copy(z_send.at[0], z_rcv.at[place * 2 + t], DL_Z + place * 2 + t, DL_Z + place * 2 + t, sib))
-                else:
-                    dl_z_in.append(copy(z_send.at[0], z_rcv.at[other], DL_Z, DL_Z, sib))
-
-    query_grad(2, False)
-    start(dq_x[1])
-    query_grad(1, False)
-    start(dq_x[0])
-    along_z(0)
-    query_grad(3, False)
-    start(dq_x[2])
-    query_grad(0, True)
-
-    for zz in range(4):
-        for xx in range(4):
-            for cc in range(2):
-                r0 = ((zz * 4 + xx) * 2 + cc) * 16
-                dw_f[cc, xx, zz] = dw_acc[r0:r0 + 16, :]
-                dw_send[cc, xx, zz] = dw_acc[r0:r0 + 16, :].astype(BF16)
-    dw_cc = copy(dw_send.at[1 - c], dw_c, DW_C, DW_C, sib)
-    start(dw_cc)
-    along_z(1)
+    arrive(*dl_w_in)
+    v = y_f[0, far_y, pl.ds(pl.multiple_of(zl * 64, 64), 64), :] + w_rcv[other].astype(F32)
+    for i in range(2, 8):
+        v = v + w_rcv[i].astype(F32)
+    far_send[...] = v.astype(BF16)
+    far_copy = copy(far_send, far_rcv, DL_FAR, DL_FAR, dev(z, x, y + 2, c))
+    start(far_copy)
 
     def to_heads(buf, base):
         come = []
@@ -462,29 +487,9 @@
             come.append(copy(buf.at[head], buf.at[src], base + j, base + j, target))
         return come
 
-    arrive(dw_cc)
-    v = dw_f[c] + dw_c[...].astype(F32)
-    dw_xf[...] = v
-    dw_xs[...] = v.astype(BF16)
-    dw_x = [copy(dw_xs.at[(x + d) % 4], dw_xr.at[d - 1], DW_X + d, DW_X + d, dev(z, x + d, y, c)) for d in range(1, 4)]
-    start(dw_x[1], dw_x[0], dw_x[2])
-
     arrive(*dr_zz)
     dr_g[head] = dr_f[0] + dr_z[0] + dr_z[1] + dr_z[2]
     dr_come = to_heads(dr_g, DR_G)
-
-    arrive(*dq_x)
-    v = dq_own[...]
-    for d in range(3):
-        v = v + dq_rcv[d].astype(F32)
-    dq_out[...] = jnp.transpose(v).astype(BF16)
-
-    arrive(*dl_z_in)
-    v = z_f[zl] + z_rcv[other].astype(F32)
-    for i in range(2, 8):
-        v = v + z_rcv[i].astype(F32)
-    ag[head] = v.astype(BF16)
-    dl_come = to_heads(ag, DL_G)
 
     arrive(*dw_x)
     v = dw_xf[x]
@@ -494,6 +499,20 @@
     dw_zs[...] = v.astype(BF16)
     dw_z = [copy(dw_zs.at[(zh + d) % 4], dw_zr.at[d - 1], DW_Z + d, DW_Z + d, dev(z + 2 * d, x, y, c)) for d in range(1, 4)]
     start(dw_z[1], dw_z[0], dw_z[2])
+
+    arrive(*dl_z_in)
+    arrive(far_copy)
+    v = z_f[zl] + z_rcv[other].astype(F32) + far_rcv[...].astype(F32)
+    for i in range(2, 8):
+        v = v + z_rcv[i].astype(F32)
+    ag[head] = v.astype(BF16)
+    dl_come = to_heads(ag, DL_G)
+
+    arrive(*dq_x)
+    v = dq_own[...]
+    for d in range(3):
+        v = v + dq_rcv[d].astype(F32)
+    dq_out[...] = jnp.transpose(v).astype(BF16)
 
     arrive(*dr_come)
     drope_out[...] = dr_g[...]
@@ -528,12 +547,13 @@
         vm((NQ, AUG, ROWS), BF16), vm((NQ, ROWS, R), BF16), vm((NQ, R, ROWS), BF16), vm((NQ, ROWS, R), BF16),
         vm((2, 4, TOK, NQ * ROWS), F32), vm((2, 4, TOK, NQ * ROWS), F32),
         vm((2, 4, TOK, NQ * ROWS), BF16), vm((2, 4, TOK, NQ * ROWS), BF16),
-        vm((NQ, 8, ROWS), F32), vm((8, ROWS), F32), vm((3, 8, ROWS), F32), vm((NQ, 8, ROWS), F32),
+        vm((4, NQ, 8, ROWS), F32), vm((8, ROWS), F32), vm((3, 8, ROWS), F32), vm((NQ, 8, ROWS), F32),
         vm((2, 2 * TOK, R), BF16), vm((2, 2 * TOK, R), BF16),
         vm((2, 4, 2 * TOK, 128), F32), vm((2, 4, 2 * TOK, 128), BF16), vm((2, 3, 2 * TOK, 128), BF16),
         vm((2, 64, 128), F32), vm((8, 64, 128), BF16), vm((8, 64, 128), BF16), vm((8, 64, 128), BF16),
-        vm((AUG, ROWS), BF16), vm((NQ, wide, TOK), BF16), vm((wide, TOK), F32), vm((3, wide, TOK), BF16),
-        vm((R, wide), F32), vm((2, 4, 4, 16, wide), F32), vm((2, 4, 4, 16, wide), BF16),
+        vm((64, 128), BF16), vm((64, 128), BF16), vm((8, 64, 128), BF16),
+        vm((LH, AUG, NQ * TOK), BF16), vm((NQ, wide, TOK), BF16), vm((wide, TOK), F32), vm((3, wide, TOK), BF16),
+        vm((2, 4, 4, 16, wide), F32), vm((2, 4, 4, 16, wide), BF16),
         vm((4, 4, 16, wide), BF16), vm((4, 4, 16, wide), F32), vm((4, 4, 16, wide), BF16),
         vm((3, 4, 16, wide), BF16), vm((4, 16, wide), F32), vm((4, 16, wide), BF16),
         vm((3, 16, wide), BF16),

time: 61.8 us -> 61.2 us (level)
  the two profiles are of different devices: /device:TPU:32 before, /device:TPU:1 now
where the time goes in v3:
time: 61.2 us; the launch traced here: 61.1 us
  Pallas kernels  60.4 us (99%)
  between operations  0.64 us (1%)
    pallas_call x1, Pallas kernels, on_device(): pl.pallas_call(kernel, out_shape=(jax.ShapeDtypeStruct((TOK, wide), BF16)...  58.6 us
    pallas_call x1, Pallas kernels, on_device(): pl.pallas_call(finish, out_shape=(jax.ShapeDtypeStruct((TOK, wide), BF16)...  1.8 us

profile of v3, /device:TPU:1, one launch (start us, length us, event | category | flops | bytes accessed | tf_op | source)
XLA Modules:
  0.0 61.1 jit_solution(18224005300652774465)
XLA Ops:
  0.6 58.6 %latent_attention_grad.1 = (bf16[128,512]{1,0:T(8,128)(2,1)}, bf16[8,64,128]{2,1,0:T(8,128)(2,1)}, f32[8,16,128]{2,1,0:T(8,128)}, f32[16,512]{1,0:T(8,128)}) custom-call(s32[32]{0:T(128)} %bo.1, bf16[128,512]{1,0:T(8,128)(2,1)} %q_in.1, bf16[128,512]{1,0:T(8,128)(2,1)} %lat_in.1, bf16[128,128]{1,0:T(8,128)(2,1)} %rope_in.1, bf16[448,512]{1,0:T(8,128)(2,1)} %bitcast.1, ...), custom_call_target="tpu_custom_call" | custom-call | tf_op jit(solution)/shard_map/latent_attention_grad/pallas_call | solution.py:566
  59.3 1.8 %finish.1 = (bf16[128,512]{1,0:T(8,128)(2,1)}, f32[128,512]{1,0:T(8,128)}, f32[128,128]{1,0:T(8,128)}, f32[16,448]{1,0:T(8,128)}) custom-call(bf16[128,512]{1,0:T(8,128)(2,1)} %get-tuple-element.8.dq_in, bf16[8,64,128]{2,1,0:T(8,128)(2,1)} %get-tuple-element.9.ag, f32[8,16,128]{2,1,0:T(8,128)} %get-tuple-element.10.dr_g, f32[16,512]{1,0:T(8,128)} %get-tuple-element.11.dw_in), custom_call_target="tpu_custom_call" | custom-call | tf_op jit(solution)/shard_map/finish/pallas_call | solution.py:582
